TPU v7x, 128 devices: a whole 4x4x4 slice. The times are simulated.
128 devices in a mesh: region: 16 (over y, x), tm: 8 (over z, core).
Axes of the slice: x: 4, y: 4, z: 4, core: 2. Of those that a mesh axis runs over, the one named last changes fastest.
Arguments:
- jacobian: bfloat16 [98304, 2048], P(('region', 'tm')), may hold values from -0.375 to 0.375
- foot_block: int32 [98304], P(('region', 'tm')), may hold values from 0 to 127, as said below
- foot_time: int32 [98304], P(('region', 'tm')), may hold values from 0 to 432, as said below
- obs_weight: bfloat16 [98304], P(('region', 'tm')), may hold values from 0.29882812 to 3
- misfit: bfloat16 [98304], P(('region', 'tm')), may hold values from -6 to 6
- kept_list: int32 [65536], P(('region', 'tm')), may hold values from 0 to 767, as said below
- kept_count: int32 [128], P(('region', 'tm')), may hold values from 256 to 512, as said below
- prior_std: float32 [448, 128, 128], P('tm', 'region'), may hold values from 0.4 to 11
- time_factor: float32 [448, 448], replicated, may hold values from -0.3 to 1.3
Outputs:
- solution: float32 [448, 128, 128], P('tm', 'region')
- residual: float32 [448, 128, 128], P('tm', 'region')
Inputs may be any that keep to these rules, and one draw needn't show every extreme that they name: `kept_list`: the 512 entries of one device are distinct row numbers within that device's own 768 rows. A device keeps the rows named by the first kept_count entries of its list. Region block of the footprint; the block is owned by the region index foot_block // 8. A footprint covers steps foot_time to foot_time + 15, all in the time window foot_time // 56: foot_time % 56 <= 40. Among the kept rows of one device, at most 6 have footprints owned by any one device (region index foot_block // 8, time index foot_time // 56); in every draw some owning device gets exactly 6 kept rows from every device.
All inputs are finite; a program needn't handle non-finite values.
Results may differ from a plain program's by a relative error of at most 0.0004.
Values may be sent and summed in bfloat16 or wider, within the bound.
A program may use at most 128 MiB of HBM per device.

v0:
```python
import jax
import jax.numpy as jnp
from jax import lax
from jax.sharding import PartitionSpec as P

ITERS = 2


def conjugate(rhs, operator, inner):
    solution = jnp.zeros_like(rhs)
    residual = rhs
    direction = rhs
    norm_now = inner(residual, residual)
    for iteration in range(ITERS):
        image = operator(direction)
        alpha = norm_now / inner(direction, image)
        solution = solution + alpha * direction
        residual = residual - alpha * image
        norm_next = inner(residual, residual)
        direction = residual + norm_next / norm_now * direction
        norm_now = norm_next
    return (solution, residual)


def local(
    jacobian,
    foot_block,
    foot_time,
    obs_weight,
    misfit,
    kept_list,
    kept_count,
    prior_std,
    time_factor,
):
    time_dev, reg_dev, cell_count = prior_std.shape
    region_count = lax.axis_size("region")
    window_count = lax.axis_size("tm")
    devices = region_count * window_count
    keep_rows = kept_list.shape[0]
    lag_cells = jacobian.shape[1]
    lag_steps = lag_cells // cell_count
    capacity = 3 * keep_rows // (2 * devices)
    total_slots = devices * capacity
    own_start = lax.axis_index("tm") * time_dev
    chosen = jacobian[kept_list]
    blocks = foot_block[kept_list]
    starts = foot_time[kept_list]
    is_kept = jnp.arange(keep_rows, dtype=jnp.int32) < kept_count[0]
    target = blocks // reg_dev * window_count + starts // time_dev
    onehot = (
        (target[:, None] == jnp.arange(devices, dtype=jnp.int32)[None, :]) & is_kept[:, None]
    ).astype(jnp.int32)
    slot_rank = jnp.sum(jnp.cumsum(onehot, axis=0) * onehot, axis=1) - 1
    position = jnp.where(is_kept, target * capacity + slot_rank, total_slots)
    placing = jnp.stack([blocks % reg_dev, starts % time_dev], axis=1)
    labels = jnp.stack([obs_weight[kept_list], misfit[kept_list]], axis=1)
    rows_out = (
        jnp.zeros((total_slots, lag_cells), jnp.bfloat16).at[position].set(chosen, mode="drop")
    )
    place_out = jnp.zeros((total_slots, 2), jnp.int32).at[position].set(placing, mode="drop")
    label_out = jnp.zeros((total_slots, 2), jnp.bfloat16).at[position].set(labels, mode="drop")
    rows_in, place_in, label_in = (
        lax.all_to_all(rows_out, ("region", "tm"), split_axis=0, concat_axis=0, tiled=True),
        lax.all_to_all(place_out, ("region", "tm"), split_axis=0, concat_axis=0, tiled=True),
        lax.all_to_all(label_out, ("region", "tm"), split_axis=0, concat_axis=0, tiled=True),
    )
    shaped = rows_in.reshape(total_slots, lag_steps, cell_count)
    index = (
        place_in[:, 1:2] + jnp.arange(lag_steps, dtype=jnp.int32)[None, :]
    ) * reg_dev + place_in[:, 0:1]
    weight_in = label_in[:, 0].astype(jnp.float32)
    misfit_in = label_in[:, 1].astype(jnp.float32)

    def observe(field):
        slab = field.reshape(time_dev * reg_dev, cell_count)[index]
        return jnp.sum(shaped.astype(jnp.float32) * slab, axis=(1, 2))

    def spread(values):
        terms = shaped.astype(jnp.float32) * values[:, None, None]
        flat = jnp.zeros((time_dev * reg_dev, cell_count), jnp.float32).at[index].add(terms)
        return flat.reshape(time_dev, reg_dev, cell_count)

    def sounding_term(field):
        return spread(weight_in * observe(field))

    source_term = spread(weight_in * misfit_in)

    def narrow(field):
        piece = lax.all_gather(field, "tm", axis=0, tiled=True)
        block = lax.dynamic_slice(time_factor, (own_start, 0), (time_dev, piece.shape[0]))
        total = jnp.dot(
            block,
            piece.reshape(piece.shape[0], reg_dev * cell_count),
            precision=lax.Precision.HIGHEST,
        )
        return prior_std * total.reshape(time_dev, reg_dev, cell_count)

    def widen(values):
        scaled = (prior_std * values).reshape(time_dev, reg_dev * cell_count)
        block = lax.dynamic_slice(
            time_factor, (own_start, 0), (time_dev, lax.axis_size("tm") * time_dev)
        )
        total = lax.psum_scatter(
            jnp.dot(block.T, scaled, precision=lax.Precision.HIGHEST),
            "tm",
            scatter_dimension=0,
            tiled=True,
        )
        return total.reshape(time_dev, reg_dev, cell_count)

    def inner(first, second):
        return lax.psum(jnp.sum(first * second), ("region", "tm"))

    def operator(field):
        return field + widen(sounding_term(narrow(field)))

    return conjugate(widen(source_term), operator, inner)


def solution(mesh):
    return jax.shard_map(
        local,
        mesh=mesh,
        in_specs=(
            P(("region", "tm"), None),
            P(("region", "tm")),
            P(("region", "tm")),
            P(("region", "tm")),
            P(("region", "tm")),
            P(("region", "tm")),
            P(("region", "tm")),
            P("tm", "region", None),
            P(),
        ),
        out_specs=(P("tm", "region", None), P("tm", "region", None)),
        check_vma=False,
    )
```

profile of v0, /device:TPU:1, one launch (start us, length us, event | category | flops | bytes accessed | tf_op | source)
XLA Modules:
  0.0 843.0 jit_solution(3517729044905587137)
XLA Ops:
  8.0 0.8 compare_select_fusion.3
  8.8 3.7 gather_fusion.3
  12.5 3.7 gather_fusion.2
  16.2 3.4 gather_fusion
  19.6 2.3 gather_fusion.1
  22.1 0.8 copy.39
  22.9 0.3 fusion.16
  23.4 0.3 fusion.15
  23.7 2.2 scatter_custom_fusion.2
  26.0 0.2 all_to_all.27
  26.2 0.7 copy.41
  26.9 12.0 %all-to-all-start.2 = ((bf16[128,6,2]{1,2,0:T(2,128)(2,1)}), bf16[128,6,2]{1,2,0:T(2,128)(2,1)}, u32[]{:S(2)}, u32[]{:S(2)}) async-start(bf16[128,6,2]{1,2,0:T(2,128)(2,1)} %copy.41), calls=%async_computation.2 | async-start | bytes 131072 | tf_op jit(solution)/shard_map/all_to_all | solution.py:66
  38.9 0.8 copy.35
  39.7 2.2 scatter_custom_fusion
  41.9 0.1 copy.36
  42.1 0.2 all_to_all.22
  42.2 0.8 copy.37
  43.0 5.2 all-to-all-done.2
  48.2 4.9 all-to-all-start
  53.1 12.3 %scatter_custom_fusion.1 = bf16[768,2048]{1,0:T(8,128)(2,1)} fusion(s32[512]{0:T(512)S(1)} %bitcast.169, bf16[768,2048]{1,0:T(8,128)(2,1)S(1)} %copy-done, s32[1024]{0:T(1024)S(1)} %pad_clamp_fusion, bf16[]{:T(256)} %constant.71.clone.1), kind=kCustom, calls=%fused_computation.18 | custom fusion | bytes 3145730 | tf_op jit(solution)/shard_map/scatter | solution.py:59
  65.4 6.3 all_to_all.25
  71.6 10.3 %all-to-all-start.1 = ((bf16[128,6,2048]{2,1,0:T(8,128)(2,1)}), bf16[128,6,2048]{2,1,0:T(8,128)(2,1)}, u32[]{:S(2)}, u32[]{:S(2)}) async-start(bf16[128,6,2048]{2,1,0:T(8,128)(2,1)} %all_to_all.25), calls=%async_computation.1 | async-start | bytes 8388608 | tf_op jit(solution)/shard_map/all_to_all | solution.py:64
  82.0 0.9 copy.42
  82.9 0.1 all_to_all.29
  83.3 0.3 compare_select_fusion
  83.5 0.2 reshape.466
  83.7 50.9 %all-to-all-done.1 = bf16[128,6,2048]{2,1,0:T(8,128)(2,1)} async-done(((bf16[128,6,2048]{2,1,0:T(8,128)(2,1)}), bf16[128,6,2048]{2,1,0:T(8,128)(2,1)}, u32[]{:S(2)}, u32[]{:S(2)}) %all-to-all-start.1) | async-done | bytes 3145760 | tf_op jit(solution)/shard_map/all_to_all | solution.py:64
  134.6 8.2 reshape.381
  142.7 5.8 broadcast_multiply_fusion.2
  148.6 66.0 %scatter_custom_fusion.3 = f32[448,128]{1,0:T(8,128)S(1)} fusion(s32[12288]{0:T(1024)S(1)} %reshape.466, f32[12288,128]{1,0:T(8,128)} %bitcast.149, f32[]{:T(128)} %constant.62.clone.1), kind=kCustom, calls=%fused_computation.79 | custom fusion | flops 1572864 | bytes 229888 | tf_op jit(solution)/shard_map/scatter-add | solution.py:81
  214.7 2.9 fusion.32
  217.6 26.6 %reduce-scatter.4.cloned.1.call-done = f32[56,1024]{1,0:T(8,128)} async-done(((f32[448,1024]{1,0:T(8,128)}), f32[56,1024]{1,0:T(8,128)}) %reduce-scatter.4.cloned.1.call-update) | async-done | bytes 229392 | tf_op jit(solution)/shard_map/reduce_scatter | solution.py:104
  244.3 1.7 copy.52
  246.0 0.4 reduce-scatter.6.cloned.1.call-start
  246.4 27.4 %all-gather.3.cloned.1.call-done = f32[448,8,128]{2,1,0:T(8,128)} async-done(((f32[56,8,128]{2,1,0:T(8,128)}), f32[448,8,128]{2,1,0:T(8,128)}) %all-gather.3.cloned.1.call-update) | async-done | bytes 1835024 | tf_op jit(solution)/shard_map/all_gather | solution.py:90
  273.8 2.9 fusion.9
  276.8 41.0 %gather_fusion.4 = f32[12288,128]{1,0:T(8,128)} fusion(f32[448,128]{1,0:T(8,128)S(1)} %bitcast.147, s32[12288]{0:T(1024)S(1)} %broadcast_clamp_fusion), kind=kCustom, calls=%fused_computation.5 | custom fusion | bytes 12632064 | tf_op jit(solution)/shard_map/gather | solution.py:76
  317.9 8.2 gather.37
  326.1 5.7 multiply_reduce_fusion.1
  332.0 5.8 broadcast_multiply_fusion.1
  337.7 66.1 %scatter_custom_fusion.4 = f32[448,128]{1,0:T(8,128)S(1)} fusion(s32[12288]{0:T(1024)S(1)} %reshape.466, f32[12288,128]{1,0:T(8,128)} %bitcast.150, f32[]{:T(128)} %constant.62.clone.1), kind=kCustom, calls=%fused_computation.77 | custom fusion | flops 1572864 | bytes 229888 | tf_op jit(solution)/shard_map/scatter-add | solution.py:81
  403.9 2.9 fusion.29
  406.8 30.1 %reduce-scatter.6.cloned.1.call-done = f32[56,1024]{1,0:T(8,128)} async-done(((f32[448,1024]{1,0:T(8,128)}), f32[56,1024]{1,0:T(8,128)}) %reduce-scatter.6.cloned.1.call-update) | async-done | bytes 229392 | tf_op jit(solution)/shard_map/reduce_scatter | solution.py:104
  437.0 1.7 multiply_reduce_fusion.3
  438.7 67.6 %all-reduce = (f32[]{:T(128)}, f32[]{:T(128)}) all-reduce(f32[]{:T(128)} %get-tuple-element.3, f32[]{:T(128)} %get-tuple-element.2), channel_id=1, replica_groups=mesh['region'=16,'tm'=8] {'region','tm'}, use_global_device_ids=true, to_apply=%region_9.10 | all-reduce | flops 2 | bytes 16 | tf_op jit(solution)/shard_map/psum | solution.py:113
  507.6 0.7 multiply_reduce_fusion.2
  508.3 1.0 copy.55
  509.2 62.6 %psum.30 = f32[]{:T(128)} all-reduce(f32[]{:T(128)} %multiply_reduce_fusion.2), channel_id=1, replica_groups=mesh['region'=16,'tm'=8] {'region','tm'}, use_global_device_ids=true, to_apply=%region_16.17 | all-reduce | flops 1 | bytes 8 | tf_op jit(solution)/shard_map/psum | solution.py:113
  573.2 0.7 multiply_add_fusion.1
  574.0 0.2 reduce-scatter.8.cloned.1.call-start
  574.2 22.8 %all-gather.5.cloned.1.call-done = f32[448,8,128]{2,1,0:T(8,128)} async-done(((f32[56,8,128]{2,1,0:T(8,128)}), f32[448,8,128]{2,1,0:T(8,128)}) %all-gather.5.cloned.1.call-update) | async-done | bytes 1835024 | tf_op jit(solution)/shard_map/all_gather | solution.py:90
  597.0 2.9 fusion.12
  600.0 41.0 %gather_fusion.5 = f32[12288,128]{1,0:T(8,128)} fusion(f32[448,128]{1,0:T(8,128)S(1)} %bitcast.146, s32[12288]{0:T(1024)S(1)} %broadcast_clamp_fusion), kind=kCustom, calls=%fused_computation.6 | custom fusion | bytes 12632064 | tf_op jit(solution)/shard_map/gather | solution.py:76
  641.1 8.2 gather.39
  649.3 5.7 multiply_reduce_fusion
  655.2 6.0 broadcast_multiply_fusion
  661.2 66.6 %scatter_custom_fusion.5 = f32[448,128]{1,0:T(8,128)} fusion(s32[12288]{0:T(1024)S(1)} %reshape.466, f32[12288,128]{1,0:T(8,128)} %bitcast.148, f32[]{:T(128)} %constant.62.clone.1), kind=kCustom, calls=%fused_computation.75 | custom fusion | flops 1572864 | bytes 229888 | tf_op jit(solution)/shard_map/scatter-add | solution.py:81
  727.8 1.0 bitcast_multiply_fusion
  728.8 3.8 fusion.24
  732.6 30.2 %reduce-scatter.8.cloned.1.call-done = f32[56,1024]{1,0:T(8,128)} async-done(((f32[448,1024]{1,0:T(8,128)}), f32[56,1024]{1,0:T(8,128)}) %reduce-scatter.8.cloned.1.call-update) | async-done | bytes 229392 | tf_op jit(solution)/shard_map/reduce_scatter | solution.py:104
  762.8 1.8 fusion.21
  764.6 67.5 %psum.31 = f32[]{:T(128)} all-reduce(f32[]{:T(128)} %fusion.21), channel_id=1, replica_groups=mesh['region'=16,'tm'=8] {'region','tm'}, use_global_device_ids=true, to_apply=%region_21.22 | all-reduce | flops 1 | bytes 8 | tf_op jit(solution)/shard_map/psum | solution.py:113
  833.5 1.0 copy.58
  834.5 1.8 fusion.23
  (62 shorter events, 1.3 us)
Async XLA Ops:
  7.2 45.9 %copy-start = (bf16[768,2048]{1,0:T(8,128)(2,1)S(1)}, bf16[768,2048]{1,0:T(8,128)(2,1)}, u32[]{:S(2)}) copy-start(bf16[768,2048]{1,0:T(8,128)(2,1)} %param.9) | copy-start | bytes 9437188
  7.2 12.4 %copy-start.2 = (s32[768]{0:T(1024)S(1)}, s32[768]{0:T(1024)}, u32[]{:S(2)}) copy-start(s32[768]{0:T(1024)} %param.11) | copy-start | bytes 9220
  26.9 21.3 %all-to-all-start.2 = ((bf16[128,6,2]{1,2,0:T(2,128)(2,1)}), bf16[128,6,2]{1,2,0:T(2,128)(2,1)}, u32[]{:S(2)}, u32[]{:S(2)}) async-start(bf16[128,6,2]{1,2,0:T(2,128)(2,1)} %copy.41), calls=%async_computation.2 | async-start | bytes 131072 | tf_op jit(solution)/shard_map/all_to_all | solution.py:66
  48.2 23.5 %all-to-all-start = ((s32[128,6,2]{1,2,0:T(2,128)}), s32[128,6,2]{1,2,0:T(2,128)S(1)}, u32[]{:S(2)}, u32[]{:S(2)}) async-start(s32[128,6,2]{1,2,0:T(2,128)} %copy.37), calls=%async_computation | async-start | bytes 262144 | tf_op jit(solution)/shard_map/all_to_all | solution.py:65
  71.6 62.9 %all-to-all-start.1 = ((bf16[128,6,2048]{2,1,0:T(8,128)(2,1)}), bf16[128,6,2048]{2,1,0:T(8,128)(2,1)}, u32[]{:S(2)}, u32[]{:S(2)}) async-start(bf16[128,6,2048]{2,1,0:T(8,128)(2,1)} %all_to_all.25), calls=%async_computation.1 | async-start | bytes 8388608 | tf_op jit(solution)/shard_map/all_to_all | solution.py:64
  82.0 162.3 %reduce-scatter.4.cloned.1.call-start = ((), (), s32[]{:S(2)}) async-start(), calls=%async_computation.6 | async-start | bytes 2064384 | tf_op jit(solution)/shard_map/reduce_scatter | solution.py:104
  142.7 71.9 %copy-start.3 = (f32[56,8,128]{2,1,0:T(8,128)S(1)}, f32[56,8,128]{2,1,0:T(8,128)}, u32[]{:S(2)}) copy-start(f32[56,8,128]{2,1,0:T(8,128)} %param.16) | copy-start | bytes 688132
  142.7 71.9 %copy-start.9 = (f32[448,448]{1,0:T(8,128)S(1)}, f32[448,448]{1,0:T(8,128)}, u32[]{:S(2)}) copy-start(f32[448,448]{1,0:T(8,128)} %param.17) | copy-start | bytes 2408452
  217.6 56.2 %all-gather.3.cloned.1.call-start = ((), (), s32[]{:S(2)}) async-start(), calls=%async_computation.7 | async-start | bytes 2064384 | tf_op jit(solution)/shard_map/all_gather | solution.py:90
  246.0 191.0 %reduce-scatter.6.cloned.1.call-start = ((), (), s32[]{:S(2)}) async-start(), calls=%async_computation.8 | async-start | bytes 2064384 | tf_op jit(solution)/shard_map/reduce_scatter | solution.py:104
  337.7 99.2 %copy-start.6 = (f32[56,1024]{1,0:T(8,128)S(1)}, f32[56,1024]{1,0:T(8,128)}, u32[]{:S(2)}) copy-start(f32[56,1024]{1,0:T(8,128)} %reduce-scatter.4.cloned.1.call-done) | copy-start | bytes 688132
  337.7 235.5 %copy-start.4 = (f32[7,8,8,128]{3,2,1,0:T(8,128)S(1)}, f32[7,8,8,128]{3,2,1,0:T(8,128)}, u32[]{:S(2)}) copy-start(f32[7,8,8,128]{3,2,1,0:T(8,128)} %copy.52) | copy-start | bytes 688132
  406.8 190.3 %all-gather.5.cloned.1.call-start = ((), (), s32[]{:S(2)}) async-start(), calls=%async_computation.9 | async-start | bytes 2064384 | tf_op jit(solution)/shard_map/all_gather | solution.py:90
  438.7 202.4 %copy-start.8 = (f32[56,1024]{1,0:T(8,128)}, f32[56,1024]{1,0:T(8,128)S(1)}, u32[]{:S(2)}) copy-start(f32[56,1024]{1,0:T(8,128)S(1)} %get-tuple-element.10) | copy-start | bytes 688132
  509.2 131.9 %copy-start.7 = (f32[7,8,8,128]{3,2,1,0:T(8,128)}, f32[7,8,8,128]{3,2,1,0:T(8,128)S(1)}, u32[]{:S(2)}) copy-start(f32[7,8,8,128]{3,2,1,0:T(8,128)S(1)} %copy.55) | copy-start | bytes 688132
  574.0 188.9 %reduce-scatter.8.cloned.1.call-start = ((), (), s32[]{:S(2)}) async-start(), calls=%async_computation.10 | async-start | bytes 2064384 | tf_op jit(solution)/shard_map/reduce_scatter | solution.py:104
  655.2 181.1 %copy-start.1 = (bf16[768,2048]{1,0:T(8,128)(2,1)S(1)}, bf16[768,2048]{1,0:T(8,128)(2,1)}, u32[]{:S(2)}) copy-start(bf16[768,2048]{1,0:T(8,128)(2,1)} %param.9) | copy-start | bytes 9437188
  728.8 105.7 %copy-start.5 = (f32[7,8,8,128]{3,2,1,0:T(8,128)S(1)}, f32[7,8,8,128]{3,2,1,0:T(8,128)}, u32[]{:S(2)}) copy-start(f32[7,8,8,128]{3,2,1,0:T(8,128)} %copy.52) | copy-start | bytes 688132
Sparse Core Ops, SparseCore 0:
  217.7 26.5 reduce-scatter.3
  246.5 27.2 all-gather.2
  406.9 30.0 reduce-scatter.5
  574.1 22.8 all-gather.4
  732.8 30.0 reduce-scatter.7
where the time goes:
time: 851 us; the launch traced here: 843 us
  other arithmetic  237 us (28%)
  blocking collectives  198 us (23%)
  waiting for transfers between devices  193 us (23%)
  local copies, waits for them, and re-layouts  152 us (18%)
  starting transfers between devices  27.9 us (3%)
  between operations  19.1 us (2%)
  matrix products  15.5 us (2%)
    scatter-add x3, other arithmetic, spread(): jnp.zeros((time_dev * reg_dev, cell_count), jnp.float32).at[index]  199 us
    psum x3, blocking collectives, inner(): return lax.psum(jnp.sum(first * second), ('region', 'tm'))  198 us
    gather x4, local copies, waits for them, and re-layouts, observe(): slab = field.reshape(time_dev * reg_dev, cell_count)[index]  98.6 us
    reduce_scatter x3, waiting for transfers between devices, widen(): lax.psum_scatter(jnp.dot(block.T, scaled, precision=lax.Precision.HIGHEST...  87 us
    all_to_all x1, waiting for transfers between devices, local(): lax.all_to_all(rows_out, ('region', 'tm'), split_axis=0, concat_axis=0, t...  50.9 us
    all_gather x2, waiting for transfers between devices, narrow(): piece = lax.all_gather(field, 'tm', axis=0, tiled=True)  50.2 us
    mul x3, other arithmetic, spread(): terms = shaped.astype(jnp.float32) * values[:, None, None]  17.5 us
  transfers between devices with their start and end apart: 8, of which 7 were waited for; matrix products, arithmetic and copies ran while one was open for 2% of the time, Pallas kernels for 0%

commit v1 on v0

v1 whole, which is shorter than its diff:
```python
import functools

import jax
import jax.numpy as jnp
from jax import lax
from jax.experimental import pallas as pl
from jax.experimental.pallas import tpu as pltpu
from jax.sharding import PartitionSpec as P

MESH = pl.DeviceIdType.MESH
HIGH = lax.Precision.HIGHEST
F32 = jnp.float32
BF16 = jnp.bfloat16
I32 = jnp.int32

BATCHES = (
    ((0, 1), (1, 0)),
    ((0, 3), (3, 0)),
    ((1, 1), (3, 3)),
    ((1, 3), (3, 1)),
    ((1, 2), (2, 1)),
    ((3, 2), (2, 3)),
    ((0, 2), (2, 0)),
    ((2, 2), (0, 0)),
)
NT_DIMS = (((1,), (1,)), ((), ()))
TN_DIMS = (((0,), (0,)), ((), ()))


def iota(shape, axis):
    return lax.broadcasted_iota(I32, shape, axis)


def dot(a, b):
    return jnp.dot(a, b, preferred_element_type=F32)


def group_transpose(x):
    shape = x.shape
    sub, grp = iota(shape, 1), iota(shape, 2) >> 4
    for s in (1, 2, 4):
        sub_bit, lane_bit = (sub & s) != 0, (grp & s) != 0
        up = pltpu.roll(pltpu.roll(x, 8 - s, 1), 16 * s, 2)
        down = pltpu.roll(pltpu.roll(x, s, 1), 128 - 16 * s, 2)
        x = jnp.where(sub_bit == lane_bit, x, jnp.where(lane_bit, up, down))
    return x


def split(x):
    low = x - x.astype(BF16).astype(F32)
    return jnp.concatenate([x, low], axis=0).astype(BF16)


def kernel(
    jac, fb_row, ft_row, ft_col, w_row, y_row, klist, kcount, prior, factor,
    x_out, r_out,
    jp, place, order, xs, rbuf, msend, mrecv, jw,
    psend, sig, cov, key, wgt, wy, uval, ubuf, vec,
    ss, gs, scal, scal_in, osend, obuf, ptmp,
    s_sem, ms_sem, r_sem, m_sem, ps_sem, p_sem, us_sem, u_sem, cs_sem, c_sem, os_sem, o_sem, l_sem,
):
    r, m = lax.axis_index("region"), lax.axis_index("tm")
    y, x, z, c = r // 4, r % 4, m // 2, m % 2

    def region_at(dy, dx):
        return ((y + dy) % 4) * 4 + (x + dx) % 4

    def tm_at(d):
        return ((z + d // 2) % 4) * 2 + (c + d) % 2

    barrier = pltpu.get_barrier_semaphore()

    def greet(i, carry):
        o = i // 8
        pl.semaphore_signal(
            barrier, inc=1, device_id=(region_at(o // 4, o % 4), tm_at(i % 8)), device_id_type=MESH
        )
        return carry

    lax.fori_loop(1, 128, greet, 0)

    blocks, starts = fb_row[...], ft_row[...]
    window = (starts * 1171) >> 16
    offset = starts - 56 * window
    kept = jnp.sum(
        jnp.where((klist[...] == iota((512, 768), 1)) & (iota((512, 768), 0) < kcount[...]), 1.0, 0.0),
        axis=0, keepdims=True,
    )
    target = (blocks >> 3) * 8 + window
    chosen = jnp.where((iota((128, 768), 0) == target) & (kept > 0.5), 1.0, 0.0)
    before = jnp.where(iota((768, 768), 0) < iota((768, 768), 1), 1.0, 0.0).astype(BF16)
    rank = jnp.sum(chosen * dot(chosen.astype(BF16), before), axis=0, keepdims=True)
    slot = jnp.where(kept > 0.5, target * 6 + rank.astype(I32), -1)
    place[...] = jnp.where(iota((768, 768), 0) == slot, 1.0, 0.0).astype(BF16)

    row = iota((16, 768), 0)
    meta = jnp.where(row == 0, (blocks & 7).astype(F32), 0.0)
    meta = jnp.where(row == 1, offset.astype(F32), meta)
    meta = jnp.where(row == 2, w_row[...].astype(F32), meta)
    meta = jnp.where(row == 3, y_row[...].astype(F32), meta)
    meta = lax.dot_general(meta.astype(BF16), place[...], NT_DIMS, preferred_element_type=F32)
    lane = iota((1, 128), 1)
    for i in range(16):
        part = meta if i == 0 else pltpu.roll(meta, 768 - 48 * i, 1)
        part = part[:, :128]
        msend[i, 0:1, :] = jnp.where(
            lane < 64, part[0:1] * 64.0 + part[1:2], pltpu.roll(part[2:3], 64, 1)
        )
        msend[i, 1:2, :] = part[2:3] * part[3:4]

    ptmp[...] = group_transpose(prior[...])
    for i in range(8):
        psend[i] = ptmp[:, i, :]
    sig[m] = psend[m]

    def turn(i, carry):
        rows = pl.ds(pl.multiple_of(i * 16, 16), 16)
        start = ft_col[rows, :]
        rho = (start - 56 * ((start * 1171) >> 16)) & 15
        lanes = iota((16, 128), 1) >> 4
        parts = [jac[rows, l * 128 : (l + 1) * 128].astype(F32) for l in range(16)]
        for s in (1, 2, 4, 8):
            bit = jnp.broadcast_to((rho & s), (16, 128)) != 0
            parts = [jnp.where(bit, parts[(l - s) % 16], parts[l]) for l in range(16)]
        for half in range(2):
            v = parts[half * 8 : half * 8 + 8]
            for s in (1, 2, 4):
                bit = (lanes & s) != 0
                new = list(v)
                for k in range(8):
                    if k & s == 0:
                        new[k] = jnp.where(bit, pltpu.roll(v[k + s], 16 * s, 1), v[k])
                        new[k + s] = jnp.where(bit, v[k + s], pltpu.roll(v[k], 128 - 16 * s, 1))
                v = new
            for k in range(8):
                jp[k, rows, half * 128 : (half + 1) * 128] = v[k].astype(BF16)
        return carry

    lax.fori_loop(0, 48, turn, 0)

    def pick(i, carry):
        rows = dot(place[...], jp[i]).astype(BF16)
        xs[pl.ds(i * 16, 16)] = rows.reshape(16, 48, 256)
        return carry

    lax.fori_loop(0, 8, pick, 0)

    pl.semaphore_wait(barrier, 127)

    def send_prior(d, carry):
        t = tm_at(d)
        pltpu.make_async_remote_copy(
            src_ref=psend.at[t], dst_ref=sig.at[m], send_sem=ps_sem, recv_sem=p_sem,
            device_id=(r, t), device_id_type=MESH,
        ).start()
        return carry

    lax.fori_loop(1, 8, send_prior, 0)

    own = 7 * 16 + 8 + m
    local_rows = pltpu.make_async_copy(xs.at[m * 16 + r], rbuf.at[own], r_sem.at[7])
    local_meta = pltpu.make_async_copy(msend.at[r], mrecv.at[own], m_sem.at[7])
    local_rows.start()
    local_meta.start()
    for g in range(8):

        def send(d, carry, g=g, which=(0, 1)):
            t = tm_at(d)
            for k in which:
                to = region_at(*BATCHES[g][k])
                here = g * 16 + k * 8 + m
                pltpu.make_async_remote_copy(
                    src_ref=msend.at[to], dst_ref=mrecv.at[here], send_sem=ms_sem, recv_sem=m_sem.at[g],
                    device_id=(to, t), device_id_type=MESH,
                ).start()
                pltpu.make_async_remote_copy(
                    src_ref=xs.at[t * 16 + to], dst_ref=rbuf.at[here], send_sem=s_sem, recv_sem=r_sem.at[g],
                    device_id=(to, t), device_id_type=MESH,
                ).start()
            return carry

        if g < 7:
            lax.fori_loop(0, 8, send, 0)
        else:
            send(0, 0, which=(0,))
            lax.fori_loop(1, 8, send, 0)

    cov[...] = lax.dot_general(factor[...], factor[...], NT_DIMS, precision=HIGH, preferred_element_type=F32)
    oi = iota((768, 768), 0)
    order[...] = jnp.where(iota((768, 768), 1) == (oi & 15) * 48 + (oi >> 4), 1.0, 0.0).astype(BF16)

    lane_lag = iota((16, 256), 1) >> 4

    def receive(g, carry):
        batch = pl.ds(g * 16, 16)
        pltpu.make_async_copy(mrecv.at[batch], mrecv.at[batch], m_sem.at[g]).wait()
        pltpu.make_async_copy(rbuf.at[batch], rbuf.at[batch], r_sem.at[g]).wait()
        rows = dot(order[...], rbuf[batch].reshape(768, 256))
        rho = mrecv[batch, 0, :].astype(I32) & 15
        for k in range(48):
            tile = rows[k * 16 : k * 16 + 16]
            later = lane_lag < rho[:, k : k + 1]
            at = pl.ds(pl.multiple_of((k % 6) * 128 + g * 16, 16), 16)
            jw[k // 6, at, 0:256] = jnp.where(later, 0.0, tile).astype(BF16)
            jw[k // 6, at, 256:512] = jnp.where(later, tile, 0.0).astype(BF16)
        return carry

    lax.fori_loop(0, 8, receive, 0)

    first = jnp.transpose(mrecv[:, 0, :])
    second = jnp.transpose(mrecv[:, 1, :])
    code = first[0:48].astype(I32)
    key[...] = ((code & 63) >> 4) * 8 + (code >> 6)
    wgt[...] = first[64:112]
    wy[...] = second[0:48]
    pltpu.make_async_copy(sig.at[pl.ds(0, 7)], sig.at[pl.ds(0, 7)], p_sem).wait()

    rows24 = iota((24, 128), 0)

    def spread(values):
        def one(w, carry):
            cols = []
            for j in range(6):
                at = pl.ds(w * 6 + j, 1)
                cols.append(jnp.where(rows24 == key[at, :], values[at, :], 0.0))
            out = dot(split(jnp.concatenate(cols, axis=1)), jw[w])
            out = out[:24] + out[24:]
            for a in range(4):
                for h in range(2 if a < 3 else 1):
                    val = None
                    if a < 3:
                        val = out[8 * a : 8 * a + 8, h * 128 : h * 128 + 128]
                    if a > 0:
                        more = out[8 * a - 8 : 8 * a, 256 + h * 128 : 384 + h * 128]
                        val = more if val is None else val + more
                    ss[w * 7 + 2 * a + h] = val
            return carry

        lax.fori_loop(0, 8, one, 0)
        return group_transpose(ss[...]).reshape(448, 128) * sig[...].reshape(448, 128)

    def observe(g_field, phase):
        h_field = sig[...].reshape(448, 128) * jnp.dot(cov[...], g_field, precision=HIGH, preferred_element_type=F32)
        ss[...] = group_transpose(h_field.reshape(56, 8, 128))

        def one(w, carry):
            rows = []
            zero = jnp.zeros((8, 128), F32)
            for a in range(3):
                cells = [ss[w * 7 + 2 * a + h] for h in range(2)]
                for h in range(2):
                    cells.append(ss[w * 7 + 2 * a + 2 + h] if 2 * a + 2 + h < 7 else zero)
                rows.append(jnp.concatenate(cells, axis=1))
            z = lax.dot_general(split(jnp.concatenate(rows, axis=0)), jw[w], NT_DIMS, preferred_element_type=F32)
            z = z[:24] + z[24:]
            for j in range(6):
                at = pl.ds(w * 6 + j, 1)
                uval[phase, at, :] = jnp.sum(
                    jnp.where(rows24 == key[at, :], z[:, j * 128 : (j + 1) * 128], 0.0), axis=0, keepdims=True
                )
            return carry

        lax.fori_loop(0, 8, one, 0)
        ubuf[phase, m] = uval[phase]

        def send_values(d, carry):
            t = tm_at(d)
            pltpu.make_async_remote_copy(
                src_ref=uval.at[phase], dst_ref=ubuf.at[phase, m], send_sem=us_sem.at[phase], recv_sem=u_sem.at[phase],
                device_id=(r, t), device_id_type=MESH,
            ).start()
            return carry

        lax.fori_loop(1, 8, send_values, 0)
        seven = ubuf.at[phase, pl.ds(0, 7)]
        pltpu.make_async_copy(seven, seven, u_sem.at[phase]).wait()
        total = ubuf[phase, 0]
        for i in range(1, 8):
            total = total + ubuf[phase, i]
        return total

    gs[0] = spread(wy)
    u0 = observe(gs[0], 0)
    vec[0] = wgt[...] * u0
    gs[1] = spread(vec.at[0])
    v0 = observe(gs[1], 1)
    vec[1] = wgt[...] * v0

    for i, term in enumerate((wy[...] * u0, vec[0] * u0, vec[0] * v0, vec[1] * v0)):
        scal[i : i + 1, :] = jnp.sum(term, axis=0, keepdims=True)
    scal[4:8, :] = jnp.zeros((4, 128), F32)
    scal_in[r] = scal[...]

    def send_scal(i, carry):
        pltpu.make_async_remote_copy(
            src_ref=scal, dst_ref=scal_in.at[r], send_sem=cs_sem, recv_sem=c_sem,
            device_id=(region_at(i // 4, i % 4), m), device_id_type=MESH,
        ).start()
        return carry

    lax.fori_loop(1, 16, send_scal, 0)
    gs[2] = spread(vec.at[1])
    fifteen = scal_in.at[pl.ds(0, 15)]
    pltpu.make_async_copy(fifteen, fifteen, c_sem).wait()
    sums = scal_in[0]
    for i in range(1, 16):
        sums = sums + scal_in[i]
    sums = jnp.sum(sums, axis=1, keepdims=True)
    g00, g01, g11, g12 = (sums[i : i + 1, :] for i in range(4))
    a0 = g00 / (g00 + g01)
    rr1 = (1 - a0) * (1 - a0) * g00 - 2 * a0 * (1 - a0) * g01 + a0 * a0 * g11
    p, q = 1 - a0 + rr1 / g00, -a0
    a1 = rr1 / (p * p * g00 + p * (p + 2 * q) * g01 + q * (2 * p + q) * g11 + q * q * g12)
    mixed = jnp.concatenate(
        [
            (a0 + a1 * p) * gs[0] + a1 * q * gs[1],
            (1 - a0 - a1 * p) * gs[0] - (a0 + a1 * (p + q)) * gs[1] - a1 * q * gs[2],
        ],
        axis=1,
    )
    osend[...] = lax.dot_general(
        factor[...], mixed, TN_DIMS, precision=HIGH, preferred_element_type=F32
    ).reshape(8, 56, 256)

    def send_out(d, carry):
        t = tm_at(d)
        pltpu.make_async_remote_copy(
            src_ref=osend.at[t], dst_ref=obuf.at[m], send_sem=os_sem, recv_sem=o_sem,
            device_id=(r, t), device_id_type=MESH,
        ).start()
        return carry

    lax.fori_loop(1, 8, send_out, 0)
    obuf[m] = osend[m]
    seven = obuf.at[pl.ds(0, 7)]
    pltpu.make_async_copy(seven, seven, o_sem).wait()
    for k, out in ((0, x_out), (1, r_out)):
        for i in range(8):
            ptmp[:, i, :] = obuf[i, :, k * 128 : (k + 1) * 128]
        out[...] = group_transpose(ptmp[...])

    all_rows, all_meta = xs.at[pl.ds(0, 127)], mrecv.at[pl.ds(0, 127)]
    pltpu.make_async_copy(all_rows, all_rows, s_sem).wait()
    pltpu.make_async_copy(all_meta, all_meta, ms_sem).wait()
    seven = sig.at[pl.ds(0, 7)]
    pltpu.make_async_copy(seven, seven, ps_sem).wait()
    for phase in range(2):
        seven = ubuf.at[phase, pl.ds(0, 7)]
        pltpu.make_async_copy(seven, seven, us_sem.at[phase]).wait()
    pltpu.make_async_copy(fifteen, fifteen, cs_sem).wait()
    seven = obuf.at[pl.ds(0, 7)]
    pltpu.make_async_copy(seven, seven, os_sem).wait()


def local(jacobian, foot_block, foot_time, obs_weight, misfit, kept_list, kept_count, prior_std, time_factor):
    field = jax.ShapeDtypeStruct(prior_std.shape, F32)
    vmem = pl.BlockSpec(memory_space=pltpu.VMEM)
    dma = pltpu.SemaphoreType.DMA
    return pl.pallas_call(
        kernel,
        out_shape=(field, field),
        in_specs=[vmem] * 10,
        out_specs=(vmem, vmem),
        scratch_shapes=[
            pltpu.VMEM((8, 768, 256), BF16),
            pltpu.VMEM((768, 768), BF16),
            pltpu.VMEM((768, 768), BF16),
            pltpu.VMEM((128, 48, 256), BF16),
            pltpu.VMEM((128, 48, 256), BF16),
            pltpu.VMEM((16, 2, 128), F32),
            pltpu.VMEM((128, 2, 128), F32),
            pltpu.VMEM((8, 768, 512), BF16),
            pltpu.VMEM((8, 56, 128), F32),
            pltpu.VMEM((8, 56, 128), F32),
            pltpu.VMEM((448, 448), F32),
            pltpu.VMEM((48, 128), I32),
            pltpu.VMEM((48, 128), F32),
            pltpu.VMEM((48, 128), F32),
            pltpu.VMEM((2, 48, 128), F32),
            pltpu.VMEM((2, 8, 48, 128), F32),
            pltpu.VMEM((2, 48, 128), F32),
            pltpu.VMEM((56, 8, 128), F32),
            pltpu.VMEM((3, 448, 128), F32),
            pltpu.VMEM((8, 128), F32),
            pltpu.VMEM((16, 8, 128), F32),
            pltpu.VMEM((8, 56, 256), F32),
            pltpu.VMEM((8, 56, 256), F32),
            pltpu.VMEM((56, 8, 128), F32),
            dma, dma, dma((8,)), dma((8,)), dma, dma, dma((2,)), dma((2,)), dma, dma, dma, dma, dma,
        ],
        compiler_params=pltpu.CompilerParams(
            collective_id=0, has_side_effects=True, vmem_limit_bytes=48 * 2**20
        ),
    )(
        jacobian,
        foot_block.reshape(1, -1),
        foot_time.reshape(1, -1),
        foot_time.reshape(-1, 1),
        obs_weight.reshape(1, -1),
        misfit.reshape(1, -1),
        kept_list.reshape(-1, 1),
        kept_count.reshape(1, 1),
        prior_std,
        time_factor,
    )


def solution(mesh):
    rows = P(("region", "tm"))
    return jax.shard_map(
        local,
        mesh=mesh,
        in_specs=(
            P(("region", "tm"), None), rows, rows, rows, rows, rows, rows, P("tm", "region", None), P(),
        ),
        out_specs=(P("tm", "region", None), P("tm", "region", None)),
        check_vma=False,
    )
```

time: 851 us -> 130 us (0.15)
  other arithmetic: 237 us -> 0 us
  blocking collectives: 198 us -> 0 us
  waiting for transfers between devices: 193 us -> 0 us
  local copies, waits for them, and re-layouts: 152 us -> 9.8 us
  Pallas kernels: 0 us -> 118 us
  starting transfers between devices: 27.9 us -> 0 us
  between operations: 19.1 us -> 1.31 us
  matrix products: 15.5 us -> 0 us
    scatter-add x3 -> x0, other arithmetic: 199 us -> none  [spread(): jnp.zeros((time_dev * reg_dev, cell_count), jnp.float32).at[index]]
    psum x3 -> x0, blocking collectives: 198 us -> none  [inner(): return lax.psum(jnp.sum(first * second), ('region', 'tm'))]
    pallas_call x0 -> x1, Pallas kernels: none -> 118 us  [local(): pl.pallas_call(kernel, out_shape=(field, field), in_specs=[vmem] * 10, ou...]
    gather x8 -> x0, local copies, waits for them, and re-layouts: 112 us -> none  [the longest x4 98.6 us: observe(): slab = field.reshape(time_dev * reg_dev, cell_count)[index]]
    reduce_scatter x3 -> x0, waiting for transfers between devices: 87 us -> none  [widen(): lax.psum_scatter(jnp.dot(block.T, scaled, precision=lax.Precision.HIGHEST...]
    all_to_all x3 -> x0, waiting for transfers between devices: 56 us -> none  [the longest x1 50.9 us: local(): lax.all_to_all(rows_out, ('region', 'tm'), split_axis=0, concat_axis=0, t...]
    all_gather x2 -> x0, waiting for transfers between devices: 50.2 us -> none  [narrow(): piece = lax.all_gather(field, 'tm', axis=0, tiled=True)]
    all_to_all x3 -> x0, starting transfers between devices: 27.2 us -> none  [the longest x1 12 us: local(): lax.all_to_all(label_out, ('region', 'tm'), split_axis=0, concat_axis=0,...]
  transfers between devices with their start and end apart: 8 -> 0, of which waited for: 7 -> 0; matrix products, arithmetic and copies ran while one was open for 2% -> 0% of each run, Pallas kernels for 0% -> 0%
where the time goes in v1:
time: 130 us; the launch traced here: 129 us
  Pallas kernels  118 us (91%)
  local copies, waits for them, and re-layouts  9.8 us (8%)
  between operations  1.31 us (1%)
    pallas_call x1, Pallas kernels, local(): pl.pallas_call(kernel, out_shape=(field, field), in_specs=[vmem] * 10, ou...  118 us
    unnamed x8, local copies, waits for them, and re-layouts  5.38 us

profile of v1, /device:TPU:1, one launch (start us, length us, event | category | flops | bytes accessed | tf_op | source)
XLA Modules:
  0.0 129.2 jit_solution(18100965592526271470)
XLA Ops:
  1.3 0.7 reshape.25.fb_row
  2.0 0.7 reshape.28.w_row
  2.7 0.7 reshape.29.y_row
  3.3 0.7 reshape.26.ft_row
  4.0 0.8 copy.12.klist
  4.9 0.8 reshape.32.ft_col
  5.7 0.0 copy-start
  5.7 1.9 %copy-done = bf16[768,2048]{1,0:T(8,128)(2,1)S(1)} copy-done((bf16[768,2048]{1,0:T(8,128)(2,1)S(1)}, bf16[768,2048]{1,0:T(8,128)(2,1)}, u32[]{:S(2)}) %copy-start) | copy-done | bytes 3145752
  7.6 0.0 copy-start.1
  7.6 1.2 copy-done.1
  8.8 0.0 copy-start.2
  8.8 0.9 copy-done.2
  9.7 118.1 %shard_map.104 = (f32[56,8,128]{2,1,0:T(8,128)S(1)}, f32[56,8,128]{2,1,0:T(8,128)S(1)}) custom-call(bf16[768,2048]{1,0:T(8,128)(2,1)S(1)} %copy-done, s32[1,768]{1,0:T(1,128)S(1)} %reshape.25.fb_row, s32[1,768]{1,0:T(1,128)S(1)} %reshape.26.ft_row, s32[768,1]{1,0:T(8,128)S(1)} %reshape.32.ft_col, bf16[1,768]{1,0:T(2,128)(2,1)S(1)} %reshape.28.w_row, ...), custom_call_target="tpu_custom_call" | custom-call | tf_op jit(solution)/shard_map/pallas_call | solution.py:359
  127.8 0.7 copy.16
  128.5 0.7 copy.17
Async XLA Ops:
  5.7 1.9 %copy-start = (bf16[768,2048]{1,0:T(8,128)(2,1)S(1)}, bf16[768,2048]{1,0:T(8,128)(2,1)}, u32[]{:S(2)}) copy-start(bf16[768,2048]{1,0:T(8,128)(2,1)} %jac.1) | copy-start | bytes 9437188
  7.6 1.2 copy-start.1
  8.8 0.9 copy-start.2

commit v2 on v1

v2 whole, which is shorter than its diff:
```python
import jax
import jax.numpy as jnp
from jax import lax
from jax.experimental import pallas as pl
from jax.experimental.pallas import tpu as pltpu
from jax.sharding import PartitionSpec as P

MESH = pl.DeviceIdType.MESH
HIGH = lax.Precision.HIGHEST
F32 = jnp.float32
BF16 = jnp.bfloat16
I32 = jnp.int32

NT_DIMS = (((1,), (1,)), ((), ()))
TN_DIMS = (((0,), (0,)), ((), ()))


def iota(shape, axis):
    return lax.broadcasted_iota(I32, shape, axis)


def dot(a, b):
    return jnp.dot(a, b, preferred_element_type=F32)


def group_transpose(x):
    shape = x.shape
    sub, grp = iota(shape, 1), iota(shape, 2) >> 4
    for s in (1, 2, 4):
        sub_bit, lane_bit = (sub & s) != 0, (grp & s) != 0
        up = pltpu.roll(pltpu.roll(x, 8 - s, 1), 16 * s, 2)
        down = pltpu.roll(pltpu.roll(x, s, 1), 128 - 16 * s, 2)
        x = jnp.where(sub_bit == lane_bit, x, jnp.where(lane_bit, up, down))
    return x


def split(x):
    low = x - x.astype(BF16).astype(F32)
    return jnp.concatenate([x, low], axis=0).astype(BF16)


def kernel(
    small, jac_in, prior_in, factor_in,
    x_out, r_out,
    jac, prior, factor, factor_t, place, order, rho_slot, picked, xs, rbuf, msend, mrecv, jw,
    psend, sig, cov, key, wgt, wy, uval, ubuf, vec,
    ss, gs, scal, scal_in, fsend, fbuf, ptmp,
    in_sem, s_sem, ms_sem, r_sem, m_sem, ps_sem, p_sem, us_sem, u_sem, cs_sem, c_sem, fs_sem, f_sem,
):
    r, m = lax.axis_index("region"), lax.axis_index("tm")
    y, x, z, c = r // 4, r % 4, m // 2, m % 2

    def region_at(dy, dx):
        return ((y + dy) % 4) * 4 + (x + dx) % 4

    def tm_at(d):
        return ((z + d // 2) % 4) * 2 + (c + d) % 2

    jac_copy = pltpu.make_async_copy(jac_in, jac, in_sem.at[0])
    prior_copy = pltpu.make_async_copy(prior_in, prior, in_sem.at[1])
    factor_copy = pltpu.make_async_copy(factor_in, factor, in_sem.at[2])
    jac_copy.start()
    prior_copy.start()
    factor_copy.start()

    barrier = pltpu.get_barrier_semaphore()

    def greet(i, carry):
        o = i // 8
        pl.semaphore_signal(
            barrier, inc=1, device_id=(region_at(o // 4, o % 4), tm_at(i % 8)), device_id_type=MESH
        )
        return carry

    lax.fori_loop(1, 128, greet, 0)

    blocks, starts = small[0:1, :].astype(I32), small[1:2, :].astype(I32)
    window = (starts * 1171) >> 16
    offset = starts - 56 * window
    named = jnp.where(iota((768, 512), 0) == small[4:5, 0:512].astype(I32), 1.0, 0.0).astype(BF16)
    kept = lax.dot_general(jnp.ones((16, 512), BF16), named, NT_DIMS, preferred_element_type=F32)[0:1]
    target = (blocks >> 3) * 8 + window
    chosen = jnp.where((iota((128, 768), 0) == target) & (kept > 0.5), 1.0, 0.0)
    before = jnp.where(iota((768, 768), 0) < iota((768, 768), 1), 1.0, 0.0).astype(BF16)
    rank = jnp.sum(chosen * dot(chosen.astype(BF16), before), axis=0, keepdims=True)
    slot = jnp.where(kept > 0.5, target * 6 + rank.astype(I32), -1)
    place[...] = jnp.where(iota((768, 768), 0) == slot, 1.0, 0.0).astype(BF16)

    row = iota((16, 768), 0)
    meta = jnp.where(row == 0, (blocks & 7).astype(F32), 0.0)
    meta = jnp.where(row == 1, offset.astype(F32), meta)
    meta = jnp.where(row == 2, small[2:3, :], meta)
    meta = jnp.where(row == 3, small[3:4, :], meta)
    meta = jnp.where(row == 4, (offset & 15).astype(F32), meta)
    meta = lax.dot_general(meta.astype(BF16), place[...], NT_DIMS, preferred_element_type=F32)
    rho_slot[...] = lax.dot_general(
        meta.astype(BF16), jnp.where(iota((16, 128), 0) == 4, 1.0, 0.0).astype(BF16), TN_DIMS,
        preferred_element_type=F32,
    ).astype(I32)
    lane = iota((1, 128), 1)
    for i in range(16):
        part = meta if i == 0 else pltpu.roll(meta, 768 - 48 * i, 1)
        part = part[:, :128]
        msend[i, 0:1, :] = jnp.where(
            lane < 64, part[0:1] * 64.0 + part[1:2], pltpu.roll(part[2:3], 64, 1)
        )
        msend[i, 1:2, :] = part[2:3] * part[3:4]

    prior_copy.wait()
    ptmp[...] = group_transpose(prior[...])
    for i in range(8):
        psend[i] = ptmp[:, i, :]
    sig[m] = psend[m]

    jac_copy.wait()
    pl.semaphore_wait(barrier, 127)
    own = m
    local_meta = pltpu.make_async_copy(msend.at[r], mrecv.at[own], m_sem.at[0])
    local_meta.start()

    lanes = iota((16, 128), 1) >> 4

    def deliver(g, carry):
        to = [region_at(g // 4 + 2 * k, g % 4 + 2 * k) for k in range(2)]
        at = [pl.multiple_of(t * 48, 16) for t in to]
        which = jnp.concatenate([place[pl.ds(a, 48), :] for a in at], axis=0)
        for l in range(0, 2048, 256):
            picked[:, l : l + 256] = dot(which, jac[:, l : l + 256])
        for k in range(2):

            def turn(i, carry, k=k):
                rows = pl.ds(pl.multiple_of(k * 48 + i * 16, 16), 16)
                out = pl.ds(pl.multiple_of(i * 16, 16), 16)
                rho = rho_slot[pl.ds(pl.multiple_of(at[k] + i * 16, 16), 16), :]
                parts = [picked[rows, l * 128 : (l + 1) * 128] for l in range(16)]
                for s in (1, 2, 4, 8):
                    bit = (rho & s) != 0
                    parts = [jnp.where(bit, parts[(l - s) % 16], parts[l]) for l in range(16)]
                for half in range(2):
                    v = parts[half * 8 : half * 8 + 8]
                    for s in (1, 2, 4):
                        bit = (lanes & s) != 0
                        new = list(v)
                        for n in range(8):
                            if n & s == 0:
                                new[n] = jnp.where(bit, pltpu.roll(v[n + s], 16 * s, 1), v[n])
                                new[n + s] = jnp.where(bit, v[n + s], pltpu.roll(v[n], 128 - 16 * s, 1))
                        v = new
                    for n in range(8):
                        xs[g * 16 + k * 8 + n, out, half * 128 : (half + 1) * 128] = v[n].astype(BF16)
                return carry

            lax.fori_loop(0, 3, turn, 0)

        def send(k, d):
            t = tm_at(d)
            here = g * 16 + k * 8 + m
            pltpu.make_async_remote_copy(
                src_ref=msend.at[to[k]], dst_ref=mrecv.at[here], send_sem=ms_sem, recv_sem=m_sem.at[g],
                device_id=(to[k], t), device_id_type=MESH,
            ).start()
            pltpu.make_async_remote_copy(
                src_ref=xs.at[g * 16 + k * 8 + t], dst_ref=rbuf.at[here], send_sem=s_sem, recv_sem=r_sem.at[g],
                device_id=(to[k], t), device_id_type=MESH,
            ).start()

        def send_two(d, carry):
            send(0, d)
            send(1, d)
            return carry

        @pl.when(g > 0)
        def _():
            send(0, 0)

        send(1, 0)
        lax.fori_loop(1, 8, send_two, 0)
        return carry

    lax.fori_loop(0, 8, deliver, 0)
    local_rows = pltpu.make_async_copy(xs.at[own], rbuf.at[own], r_sem.at[0])
    local_rows.start()

    def send_prior(d, carry):
        t = tm_at(d)
        pltpu.make_async_remote_copy(
            src_ref=psend.at[t], dst_ref=sig.at[m], send_sem=ps_sem, recv_sem=p_sem,
            device_id=(r, t), device_id_type=MESH,
        ).start()
        return carry

    lax.fori_loop(1, 8, send_prior, 0)

    factor_copy.wait()
    cov[...] = lax.dot_general(factor[...], factor[...], NT_DIMS, precision=HIGH, preferred_element_type=F32)
    factor_t[...] = jnp.transpose(factor[...])
    oi = iota((768, 768), 0)
    order[...] = jnp.where(iota((768, 768), 1) == (oi & 15) * 48 + (oi >> 4), 1.0, 0.0).astype(BF16)

    lane_lag = iota((16, 256), 1) >> 4

    def receive(g, carry):
        batch = pl.ds(g * 16, 16)
        pltpu.make_async_copy(mrecv.at[batch], mrecv.at[batch], m_sem.at[g]).wait()
        pltpu.make_async_copy(rbuf.at[batch], rbuf.at[batch], r_sem.at[g]).wait()
        rows = dot(order[...], rbuf[batch].reshape(768, 256))
        rho = mrecv[batch, 0, :].astype(I32) & 15
        for k in range(48):
            tile = rows[k * 16 : k * 16 + 16]
            later = lane_lag < rho[:, k : k + 1]
            at = pl.ds(pl.multiple_of((k % 6) * 128 + g * 16, 16), 16)
            jw[k // 6, at, 0:256] = jnp.where(later, 0.0, tile).astype(BF16)
            jw[k // 6, at, 256:512] = jnp.where(later, tile, 0.0).astype(BF16)
        return carry

    lax.fori_loop(0, 8, receive, 0)

    first = jnp.transpose(mrecv[:, 0, :])
    second = jnp.transpose(mrecv[:, 1, :])
    code = first[0:48].astype(I32)
    key[...] = ((code & 63) >> 4) * 8 + (code >> 6)
    wgt[...] = first[64:112]
    wy[...] = second[0:48]
    pltpu.make_async_copy(sig.at[pl.ds(0, 7)], sig.at[pl.ds(0, 7)], p_sem).wait()

    rows24 = iota((24, 128), 0)

    def spread(values, ready):
        def one(w, carry):
            cols = []
            for j in range(6):
                at = pl.ds(w * 6 + j, 1)
                cols.append(jnp.where(rows24 == key[at, :], values[at, :], 0.0))
            out = dot(split(jnp.concatenate(cols, axis=1)), jw[w])
            out = out[:24] + out[24:]
            for a in range(4):
                for h in range(2 if a < 3 else 1):
                    val = None
                    if a < 3:
                        val = out[8 * a : 8 * a + 8, h * 128 : h * 128 + 128]
                    if a > 0:
                        more = out[8 * a - 8 : 8 * a, 256 + h * 128 : 384 + h * 128]
                        val = more if val is None else val + more
                    ss[w * 7 + 2 * a + h] = val
            return carry

        for half in range(2):
            ready(half)
            lax.fori_loop(half * 4, half * 4 + 4, one, 0)
        return group_transpose(ss[...]).reshape(448, 128) * sig[...].reshape(448, 128)

    def observe(g_field, phase):
        h_field = sig[...].reshape(448, 128) * jnp.dot(cov[...], g_field, precision=HIGH, preferred_element_type=F32)
        ss[...] = group_transpose(h_field.reshape(56, 8, 128))

        def one(w, carry):
            rows = []
            zero = jnp.zeros((8, 128), F32)
            for a in range(3):
                cells = [ss[w * 7 + 2 * a + h] for h in range(2)]
                for h in range(2):
                    cells.append(ss[w * 7 + 2 * a + 2 + h] if 2 * a + 2 + h < 7 else zero)
                rows.append(jnp.concatenate(cells, axis=1))
            v = lax.dot_general(split(jnp.concatenate(rows, axis=0)), jw[w], NT_DIMS, preferred_element_type=F32)
            v = v[:24] + v[24:]
            for j in range(6):
                uval[phase, pl.ds(w * 6 + j, 1), :] = jnp.sum(
                    jnp.where(rows24 == key[pl.ds(w * 6 + j, 1), :], v[:, j * 128 : (j + 1) * 128], 0.0),
                    axis=0, keepdims=True,
                )
            return carry

        for half in range(2):
            lax.fori_loop(half * 4, half * 4 + 4, one, 0)
            mine = uval.at[phase, pl.ds(half * 24, 24)]

            def send_values(d, carry, half=half, mine=mine):
                t = tm_at(d)
                pltpu.make_async_remote_copy(
                    src_ref=mine, dst_ref=ubuf.at[phase, half, m],
                    send_sem=us_sem.at[phase, half], recv_sem=u_sem.at[phase, half],
                    device_id=(r, t), device_id_type=MESH,
                ).start()
                return carry

            lax.fori_loop(1, 8, send_values, 0)
            ubuf[phase, half, m] = uval[phase, half * 24 : half * 24 + 24, :]

    def collect(phase):
        def ready(half):
            seven = ubuf.at[phase, half, pl.ds(0, 7)]
            pltpu.make_async_copy(seven, seven, u_sem.at[phase, half]).wait()
            total = ubuf[phase, half, 0]
            for i in range(1, 8):
                total = total + ubuf[phase, half, i]
            rows = slice(half * 24, half * 24 + 24)
            weighted = wgt[rows, :] * total
            vec[phase, rows, :] = weighted
            if phase == 0:
                terms = (wy[rows, :] * total, weighted * total)
            else:
                terms = (vec[0, rows, :] * total, weighted * total)
            for i, term in enumerate(terms):
                term = jnp.sum(term, axis=0, keepdims=True)
                at = slice(2 * phase + i, 2 * phase + i + 1)
                scal[at, :] = term if half == 0 else scal[at, :] + term

        return ready

    def send_field(k):
        fsend[k] = jnp.dot(
            factor_t[...], gs[k], precision=HIGH, preferred_element_type=F32
        ).reshape(8, 56, 128)

        def send(d, carry):
            t = tm_at(d)
            pltpu.make_async_remote_copy(
                src_ref=fsend.at[k, t], dst_ref=fbuf.at[k, m], send_sem=fs_sem.at[k], recv_sem=f_sem.at[k],
                device_id=(r, t), device_id_type=MESH,
            ).start()
            return carry

        lax.fori_loop(1, 8, send, 0)
        fbuf[k, m] = fsend[k, m]

    def wait_field(k):
        seven = fbuf.at[k, pl.ds(0, 7)]
        pltpu.make_async_copy(seven, seven, f_sem.at[k]).wait()

    scal[4:8, :] = jnp.zeros((4, 128), F32)
    gs[0] = spread(wy, lambda half: None)
    observe(gs[0], 0)
    send_field(0)
    gs[1] = spread(vec.at[0], collect(0))
    observe(gs[1], 1)
    send_field(1)
    gs[2] = spread(vec.at[1], collect(1))
    send_field(2)

    scal_in[r] = scal[...]

    def send_scal(i, carry):
        pltpu.make_async_remote_copy(
            src_ref=scal, dst_ref=scal_in.at[r], send_sem=cs_sem, recv_sem=c_sem,
            device_id=(region_at(i // 4, i % 4), m), device_id_type=MESH,
        ).start()
        return carry

    lax.fori_loop(1, 16, send_scal, 0)
    fifteen = scal_in.at[pl.ds(0, 15)]
    pltpu.make_async_copy(fifteen, fifteen, c_sem).wait()
    sums = scal_in[0]
    for i in range(1, 16):
        sums = sums + scal_in[i]
    sums = jnp.sum(sums, axis=1, keepdims=True)
    g00, g01, g11, g12 = (sums[i : i + 1, :] for i in range(4))
    a0 = g00 / (g00 + g01)
    rr1 = (1 - a0) * (1 - a0) * g00 - 2 * a0 * (1 - a0) * g01 + a0 * a0 * g11
    p, q = 1 - a0 + rr1 / g00, -a0
    a1 = rr1 / (p * p * g00 + p * (p + 2 * q) * g01 + q * (2 * p + q) * g11 + q * q * g12)
    wait_field(0)
    wait_field(1)
    for i in range(8):
        ptmp[:, i, :] = (a0 + a1 * p) * fbuf[0, i] + a1 * q * fbuf[1, i]
    x_out[...] = group_transpose(ptmp[...])
    for i in range(8):
        fbuf[0, i] = (1 - a0 - a1 * p) * fbuf[0, i] - (a0 + a1 * (p + q)) * fbuf[1, i]
    wait_field(2)
    for i in range(8):
        ptmp[:, i, :] = fbuf[0, i] - a1 * q * fbuf[2, i]
    r_out[...] = group_transpose(ptmp[...])

    all_rows, all_meta = xs.at[pl.ds(0, 127)], mrecv.at[pl.ds(0, 127)]
    pltpu.make_async_copy(all_rows, all_rows, s_sem).wait()
    pltpu.make_async_copy(all_meta, all_meta, ms_sem).wait()
    seven = sig.at[pl.ds(0, 7)]
    pltpu.make_async_copy(seven, seven, ps_sem).wait()
    for phase in range(2):
        for half in range(2):
            seven = ubuf.at[phase, half, pl.ds(0, 7)]
            pltpu.make_async_copy(seven, seven, us_sem.at[phase, half]).wait()
    pltpu.make_async_copy(fifteen, fifteen, cs_sem).wait()
    for k in range(3):
        seven = fbuf.at[k, pl.ds(0, 7)]
        pltpu.make_async_copy(seven, seven, fs_sem.at[k]).wait()


def local(jacobian, foot_block, foot_time, obs_weight, misfit, kept_list, kept_count, prior_std, time_factor):
    field = jax.ShapeDtypeStruct(prior_std.shape, F32)
    vmem = pl.BlockSpec(memory_space=pltpu.VMEM)
    anywhere = pl.BlockSpec(memory_space=pl.ANY)
    dma = pltpu.SemaphoreType.DMA
    pool, keep = foot_block.shape[0], kept_list.shape[0]
    named = jnp.where(jnp.arange(keep, dtype=I32) < kept_count[0], kept_list, -1)
    named = jnp.pad(named, (0, pool - keep), constant_values=-1)
    row = lax.broadcasted_iota(I32, (8, pool), 0)
    small = jnp.zeros((8, pool), F32)
    for i, values in enumerate((foot_block, foot_time, obs_weight, misfit, named)):
        small = jnp.where(row == i, values.astype(F32)[None, :], small)
    return pl.pallas_call(
        kernel,
        out_shape=(field, field),
        in_specs=[vmem] + [anywhere] * 3,
        out_specs=(vmem, vmem),
        scratch_shapes=[
            pltpu.VMEM((768, 2048), BF16),
            pltpu.VMEM((56, 8, 128), F32),
            pltpu.VMEM((448, 448), F32),
            pltpu.VMEM((448, 448), F32),
            pltpu.VMEM((768, 768), BF16),
            pltpu.VMEM((768, 768), BF16),
            pltpu.VMEM((768, 128), I32),
            pltpu.VMEM((96, 2048), F32),
            pltpu.VMEM((128, 48, 256), BF16),
            pltpu.VMEM((128, 48, 256), BF16),
            pltpu.VMEM((16, 2, 128), F32),
            pltpu.VMEM((128, 2, 128), F32),
            pltpu.VMEM((8, 768, 512), BF16),
            pltpu.VMEM((8, 56, 128), F32),
            pltpu.VMEM((8, 56, 128), F32),
            pltpu.VMEM((448, 448), F32),
            pltpu.VMEM((48, 128), I32),
            pltpu.VMEM((48, 128), F32),
            pltpu.VMEM((48, 128), F32),
            pltpu.VMEM((2, 48, 128), F32),
            pltpu.VMEM((2, 2, 8, 24, 128), F32),
            pltpu.VMEM((2, 48, 128), F32),
            pltpu.VMEM((56, 8, 128), F32),
            pltpu.VMEM((3, 448, 128), F32),
            pltpu.VMEM((8, 128), F32),
            pltpu.VMEM((16, 8, 128), F32),
            pltpu.VMEM((3, 8, 56, 128), F32),
            pltpu.VMEM((3, 8, 56, 128), F32),
            pltpu.VMEM((56, 8, 128), F32),
            dma((3,)), dma, dma, dma((8,)), dma((8,)), dma, dma, dma((2, 2)), dma((2, 2)), dma, dma, dma((3,)), dma((3,)),
        ],
        compiler_params=pltpu.CompilerParams(
            collective_id=0, has_side_effects=True, vmem_limit_bytes=48 * 2**20
        ),
    )(small, jacobian, prior_std, time_factor)


def solution(mesh):
    rows = P(("region", "tm"))
    return jax.shard_map(
        local,
        mesh=mesh,
        in_specs=(
            P(("region", "tm"), None), rows, rows, rows, rows, rows, rows, P("tm", "region", None), P(),
        ),
        out_specs=(P("tm", "region", None), P("tm", "region", None)),
        check_vma=False,
    )
```

time: 130 us -> 104 us (0.80)
  Pallas kernels: 118 us -> 92.9 us
  local copies, waits for them, and re-layouts: 9.8 us -> 5.38 us
  other arithmetic: 0 us -> 3.53 us
    pallas_call x1, Pallas kernels: 118 us -> 92.9 us  [local(): pl.pallas_call(kernel, out_shape=(field, field), in_specs=[vmem] + [anywh...]
    reshape x6 -> x0, local copies, waits for them, and re-layouts: 4.41 us -> none  [the longest x1 0.85 us: local(): foot_time.reshape(-1, 1)]
    convert_element_type x0 -> x5, other arithmetic: none -> 2.75 us  [local(): small = jnp.where(row == i, values.astype(F32)[None, :], small)]
where the time goes in v2:
time: 104 us; the launch traced here: 103 us
  Pallas kernels  92.9 us (89%)
  local copies, waits for them, and re-layouts  5.38 us (5%)
  other arithmetic  3.53 us (3%)
  between operations  1.31 us (1%)
    pallas_call x1, Pallas kernels, local(): pl.pallas_call(kernel, out_shape=(field, field), in_specs=[vmem] + [anywh...  92.9 us
    unnamed x8, local copies, waits for them, and re-layouts  5.38 us
    convert_element_type x5, other arithmetic, local(): small = jnp.where(row == i, values.astype(F32)[None, :], small)  2.75 us

profile of v2, /device:TPU:1, one launch (start us, length us, event | category | flops | bytes accessed | tf_op | source)
XLA Modules:
  0.0 103.2 jit_solution(12378403535579049519)
XLA Ops:
  1.3 0.7 fusion
  2.0 0.7 convert_element_type.19
  2.7 0.7 convert_element_type.18
  3.4 0.7 convert_element_type.17
  4.1 0.7 convert_element_type.16
  4.8 0.1 select_select_fusion.small
  4.8 0.0 copy-start
  4.8 1.9 %copy-done = bf16[768,2048]{1,0:T(8,128)(2,1)S(1)} copy-done((bf16[768,2048]{1,0:T(8,128)(2,1)S(1)}, bf16[768,2048]{1,0:T(8,128)(2,1)}, u32[]{:S(2)}) %copy-start) | copy-done | bytes 3145752
  6.7 0.0 copy-start.1
  6.7 1.2 %copy-done.1 = f32[448,448]{1,0:T(8,128)S(1)} copy-done((f32[448,448]{1,0:T(8,128)S(1)}, f32[448,448]{1,0:T(8,128)}, u32[]{:S(2)}) %copy-start.1) | copy-done | bytes 802840
  7.9 0.0 copy-start.2
  7.9 0.9 copy-done.2
  8.8 92.9 %shard_map.104 = (f32[56,8,128]{2,1,0:T(8,128)S(1)}, f32[56,8,128]{2,1,0:T(8,128)S(1)}) custom-call(f32[8,768]{1,0:T(8,128)S(1)} %select_select_fusion.small, bf16[768,2048]{1,0:T(8,128)(2,1)S(1)} %copy-done, f32[56,8,128]{2,1,0:T(8,128)S(1)} %copy-done.2, f32[448,448]{1,0:T(8,128)S(1)} %copy-done.1), custom_call_target="tpu_custom_call" | custom-call | tf_op jit(solution)/shard_map/pallas_call | solution.py:400
  101.8 0.7 copy.14
  102.5 0.7 copy.15
  (4 shorter events, 0.0 us)
Async XLA Ops:
  4.8 1.9 %copy-start = (bf16[768,2048]{1,0:T(8,128)(2,1)S(1)}, bf16[768,2048]{1,0:T(8,128)(2,1)}, u32[]{:S(2)}) copy-start(bf16[768,2048]{1,0:T(8,128)(2,1)} %jac_in.1) | copy-start | bytes 9437188
  6.7 1.2 %copy-start.1 = (f32[448,448]{1,0:T(8,128)S(1)}, f32[448,448]{1,0:T(8,128)}, u32[]{:S(2)}) copy-start(f32[448,448]{1,0:T(8,128)} %factor_in.1) | copy-start | bytes 2408452
  7.9 0.9 copy-start.2

commit v3 on v2

--- a/solution.py
+++ b/solution.py
@@ -39,13 +39,21 @@
     return jnp.concatenate([x, low], axis=0).astype(BF16)
 
 
+def in_time(pair, x):
+    n = x.shape[0]
+    high = x.astype(BF16)
+    low = (x - high.astype(F32)).astype(BF16)
+    out = dot(pair[0:n, :], jnp.concatenate([high, low], axis=1))
+    return out[:, 0:128] + out[:, 128:256] + dot(pair[n : 2 * n, :], high)
+
+
 def kernel(
-    small, jac_in, prior_in, factor_in,
+    fb_in, ft_in, w_in, y_in, list_in, count_in, jac_in, prior_in, factor_in,
     x_out, r_out,
     jac, prior, factor, factor_t, place, order, rho_slot, picked, xs, rbuf, msend, mrecv, jw,
     psend, sig, cov, key, wgt, wy, uval, ubuf, vec,
     ss, gs, scal, scal_in, fsend, fbuf, ptmp,
-    in_sem, s_sem, ms_sem, r_sem, m_sem, ps_sem, p_sem, us_sem, u_sem, cs_sem, c_sem, fs_sem, f_sem,
+    entered, in_sem, s_sem, ms_sem, r_sem, m_sem, ps_sem, p_sem, us_sem, u_sem, cs_sem, c_sem, fs_sem, f_sem,
 ):
     r, m = lax.axis_index("region"), lax.axis_index("tm")
     y, x, z, c = r // 4, r % 4, m // 2, m % 2
@@ -65,19 +73,25 @@
 
     barrier = pltpu.get_barrier_semaphore()
 
-    def greet(i, carry):
-        o = i // 8
-        pl.semaphore_signal(
-            barrier, inc=1, device_id=(region_at(o // 4, o % 4), tm_at(i % 8)), device_id_type=MESH
-        )
-        return carry
-
-    lax.fori_loop(1, 128, greet, 0)
-
-    blocks, starts = small[0:1, :].astype(I32), small[1:2, :].astype(I32)
+    def greet_group(d, carry):
+        pl.semaphore_signal(barrier, inc=1, device_id=(r, tm_at(d)), device_id_type=MESH)
+        return carry
+
+    def greet_region(i, carry):
+        pl.semaphore_signal(barrier, inc=1, device_id=(region_at(i // 4, i % 4), m), device_id_type=MESH)
+        return carry
+
+    lax.fori_loop(1, 16, greet_region, 0)
+    lax.fori_loop(1, 8, greet_group, 0)
+
+    def as_row(ref):
+        return ref[...].reshape(1, -1)
+
+    blocks, starts = as_row(fb_in), as_row(ft_in)
     window = (starts * 1171) >> 16
     offset = starts - 56 * window
-    named = jnp.where(iota((768, 512), 0) == small[4:5, 0:512].astype(I32), 1.0, 0.0).astype(BF16)
+    named = jnp.where(iota((1, 512), 1) < count_in[0], as_row(list_in), -1)
+    named = jnp.where(iota((768, 512), 0) == named, 1.0, 0.0).astype(BF16)
     kept = lax.dot_general(jnp.ones((16, 512), BF16), named, NT_DIMS, preferred_element_type=F32)[0:1]
     target = (blocks >> 3) * 8 + window
     chosen = jnp.where((iota((128, 768), 0) == target) & (kept > 0.5), 1.0, 0.0)
@@ -89,8 +103,8 @@
     row = iota((16, 768), 0)
     meta = jnp.where(row == 0, (blocks & 7).astype(F32), 0.0)
     meta = jnp.where(row == 1, offset.astype(F32), meta)
-    meta = jnp.where(row == 2, small[2:3, :], meta)
-    meta = jnp.where(row == 3, small[3:4, :], meta)
+    meta = jnp.where(row == 2, as_row(w_in).astype(F32), meta)
+    meta = jnp.where(row == 3, as_row(y_in).astype(F32), meta)
     meta = jnp.where(row == 4, (offset & 15).astype(F32), meta)
     meta = lax.dot_general(meta.astype(BF16), place[...], NT_DIMS, preferred_element_type=F32)
     rho_slot[...] = lax.dot_general(
@@ -106,6 +120,14 @@
         )
         msend[i, 1:2, :] = part[2:3] * part[3:4]
 
+    pl.semaphore_wait(barrier, 22)
+
+    def vouch(d, carry):
+        pl.semaphore_signal(entered, inc=1, device_id=(r, tm_at(d)), device_id_type=MESH)
+        return carry
+
+    lax.fori_loop(1, 8, vouch, 0)
+
     prior_copy.wait()
     ptmp[...] = group_transpose(prior[...])
     for i in range(8):
@@ -113,7 +135,7 @@
     sig[m] = psend[m]
 
     jac_copy.wait()
-    pl.semaphore_wait(barrier, 127)
+    pl.semaphore_wait(entered, 7)
     own = m
     local_meta = pltpu.make_async_copy(msend.at[r], mrecv.at[own], m_sem.at[0])
     local_meta.start()
@@ -192,8 +214,10 @@
     lax.fori_loop(1, 8, send_prior, 0)
 
     factor_copy.wait()
-    cov[...] = lax.dot_general(factor[...], factor[...], NT_DIMS, precision=HIGH, preferred_element_type=F32)
-    factor_t[...] = jnp.transpose(factor[...])
+    product = lax.dot_general(factor[...], factor[...], NT_DIMS, precision=HIGH, preferred_element_type=F32)
+    for ref, value in ((cov, product), (factor_t, jnp.transpose(factor[...]))):
+        ref[0:448, :] = value.astype(BF16)
+        ref[448:896, :] = (value - value.astype(BF16).astype(F32)).astype(BF16)
     oi = iota((768, 768), 0)
     order[...] = jnp.where(iota((768, 768), 1) == (oi & 15) * 48 + (oi >> 4), 1.0, 0.0).astype(BF16)
 
@@ -246,11 +270,11 @@
 
         for half in range(2):
             ready(half)
-            lax.fori_loop(half * 4, half * 4 + 4, one, 0)
+            [one(w, 0) for w in range(half * 4, half * 4 + 4)]
         return group_transpose(ss[...]).reshape(448, 128) * sig[...].reshape(448, 128)
 
     def observe(g_field, phase):
-        h_field = sig[...].reshape(448, 128) * jnp.dot(cov[...], g_field, precision=HIGH, preferred_element_type=F32)
+        h_field = sig[...].reshape(448, 128) * in_time(cov, g_field)
         ss[...] = group_transpose(h_field.reshape(56, 8, 128))
 
         def one(w, carry):
@@ -271,7 +295,7 @@
             return carry
 
         for half in range(2):
-            lax.fori_loop(half * 4, half * 4 + 4, one, 0)
+            [one(w, 0) for w in range(half * 4, half * 4 + 4)]
             mine = uval.at[phase, pl.ds(half * 24, 24)]
 
             def send_values(d, carry, half=half, mine=mine):
@@ -308,9 +332,7 @@
         return ready
 
     def send_field(k):
-        fsend[k] = jnp.dot(
-            factor_t[...], gs[k], precision=HIGH, preferred_element_type=F32
-        ).reshape(8, 56, 128)
+        fsend[k] = in_time(factor_t, gs[k]).reshape(8, 56, 128)
 
         def send(d, carry):
             t = tm_at(d)
@@ -388,25 +410,18 @@
 def local(jacobian, foot_block, foot_time, obs_weight, misfit, kept_list, kept_count, prior_std, time_factor):
     field = jax.ShapeDtypeStruct(prior_std.shape, F32)
     vmem = pl.BlockSpec(memory_space=pltpu.VMEM)
-    anywhere = pl.BlockSpec(memory_space=pl.ANY)
+    hbm = pl.BlockSpec(memory_space=pltpu.HBM)
     dma = pltpu.SemaphoreType.DMA
-    pool, keep = foot_block.shape[0], kept_list.shape[0]
-    named = jnp.where(jnp.arange(keep, dtype=I32) < kept_count[0], kept_list, -1)
-    named = jnp.pad(named, (0, pool - keep), constant_values=-1)
-    row = lax.broadcasted_iota(I32, (8, pool), 0)
-    small = jnp.zeros((8, pool), F32)
-    for i, values in enumerate((foot_block, foot_time, obs_weight, misfit, named)):
-        small = jnp.where(row == i, values.astype(F32)[None, :], small)
     return pl.pallas_call(
         kernel,
         out_shape=(field, field),
-        in_specs=[vmem] + [anywhere] * 3,
+        in_specs=[vmem] * 5 + [pl.BlockSpec(memory_space=pltpu.SMEM)] + [hbm] * 3,
         out_specs=(vmem, vmem),
         scratch_shapes=[
             pltpu.VMEM((768, 2048), BF16),
             pltpu.VMEM((56, 8, 128), F32),
             pltpu.VMEM((448, 448), F32),
-            pltpu.VMEM((448, 448), F32),
+            pltpu.VMEM((896, 448), BF16),
             pltpu.VMEM((768, 768), BF16),
             pltpu.VMEM((768, 768), BF16),
             pltpu.VMEM((768, 128), I32),
@@ -418,7 +433,7 @@
             pltpu.VMEM((8, 768, 512), BF16),
             pltpu.VMEM((8, 56, 128), F32),
             pltpu.VMEM((8, 56, 128), F32),
-            pltpu.VMEM((448, 448), F32),
+            pltpu.VMEM((896, 448), BF16),
             pltpu.VMEM((48, 128), I32),
             pltpu.VMEM((48, 128), F32),
             pltpu.VMEM((48, 128), F32),
@@ -432,12 +447,12 @@
             pltpu.VMEM((3, 8, 56, 128), F32),
             pltpu.VMEM((3, 8, 56, 128), F32),
             pltpu.VMEM((56, 8, 128), F32),
-            dma((3,)), dma, dma, dma((8,)), dma((8,)), dma, dma, dma((2, 2)), dma((2, 2)), dma, dma, dma((3,)), dma((3,)),
+            pltpu.SemaphoreType.REGULAR, dma((3,)), dma, dma, dma((8,)), dma((8,)), dma, dma, dma((2, 2)), dma((2, 2)), dma, dma, dma((3,)), dma((3,)),
         ],
         compiler_params=pltpu.CompilerParams(
-            collective_id=0, has_side_effects=True, vmem_limit_bytes=48 * 2**20
+            collective_id=0, has_side_effects=True, vmem_limit_bytes=60 * 2**20
         ),
-    )(small, jacobian, prior_std, time_factor)
+    )(foot_block, foot_time, obs_weight, misfit, kept_list, kept_count, jacobian, prior_std, time_factor)
 
 
 def solution(mesh):

time: 104 us -> 90.5 us (0.87)
  Pallas kernels: 92.9 us -> 85.8 us
  other arithmetic: 3.53 us -> 0 us
  local copies, waits for them, and re-layouts: 5.38 us -> 3.28 us
    pallas_call x1, Pallas kernels: 92.9 us -> 85.8 us  [local(): pl.pallas_call(kernel, out_shape=(field, field), in_specs=[vmem] * 5 + [p...]
    convert_element_type x5 -> x0, other arithmetic: 2.75 us -> none  [local(): small = jnp.where(row == i, values.astype(F32)[None, :], small)]
    unnamed x8 -> x2, local copies, waits for them, and re-layouts: 5.38 us -> 3.28 us
where the time goes in v3:
time: 90.5 us; the launch traced here: 90.3 us
  Pallas kernels  85.8 us (95%)
  local copies, waits for them, and re-layouts  3.28 us (4%)
  between operations  1.29 us (1%)
    pallas_call x1, Pallas kernels, local(): pl.pallas_call(kernel, out_shape=(field, field), in_specs=[vmem] * 5 + [p...  85.8 us
    unnamed x2, local copies, waits for them, and re-layouts  3.28 us

profile of v3, /device:TPU:1, one launch (start us, length us, event | category | flops | bytes accessed | tf_op | source)
XLA Modules:
  0.0 90.3 jit_solution(5305524908598340072)
XLA Ops:
  1.3 85.8 %shard_map.104 = (f32[56,8,128]{2,1,0:T(8,128)}, f32[56,8,128]{2,1,0:T(8,128)}) custom-call(s32[768]{0:T(1024)} %fb_in.1, s32[768]{0:T(1024)} %ft_in.1, bf16[768]{0:T(1024)(128)(2,1)} %w_in.1, bf16[768]{0:T(1024)(128)(2,1)} %y_in.1, s32[512]{0:T(512)} %list_in.1, s32[1]{0:T(128)S(6)} %copy.13.count_in, bf16[768,2048]{1,0:T(8,128)(2,1)} %jac_in.1, ...), custom_call_target="tpu_custom_call" | custom-call | tf_op jit(solution)/shard_map/pallas_call | solution.py:415
  87.1 1.6 %copy.14 = f32[56,8,128]{2,1,0:T(8,128)} copy(f32[56,8,128]{2,1,0:T(8,128)} %get-tuple-element.4) | data formatting | bytes 458752
  88.7 1.6 %copy.15 = f32[56,8,128]{2,1,0:T(8,128)} copy(f32[56,8,128]{2,1,0:T(8,128)} %get-tuple-element.5) | data formatting | bytes 458752

commit v4 on v3

--- a/solution.py
+++ b/solution.py
@@ -50,7 +50,7 @@
 def kernel(
     fb_in, ft_in, w_in, y_in, list_in, count_in, jac_in, prior_in, factor_in,
     x_out, r_out,
-    jac, prior, factor, factor_t, place, order, rho_slot, picked, xs, rbuf, msend, mrecv, jw,
+    jac, prior, factor, factor_t, slots, metas, order, rho_slot, picked, xs, rbuf, msend, mrecv, jw,
     psend, sig, cov, key, wgt, wy, uval, ubuf, vec,
     ss, gs, scal, scal_in, fsend, fbuf, ptmp,
     entered, in_sem, s_sem, ms_sem, r_sem, m_sem, ps_sem, p_sem, us_sem, u_sem, cs_sem, c_sem, fs_sem, f_sem,
@@ -91,14 +91,25 @@
     window = (starts * 1171) >> 16
     offset = starts - 56 * window
     named = jnp.where(iota((1, 512), 1) < count_in[0], as_row(list_in), -1)
-    named = jnp.where(iota((768, 512), 0) == named, 1.0, 0.0).astype(BF16)
-    kept = lax.dot_general(jnp.ones((16, 512), BF16), named, NT_DIMS, preferred_element_type=F32)[0:1]
+    high = jnp.where(iota((32, 512), 0) == (named >> 5), 1.0, 0.0).astype(BF16)
+    low = jnp.where(iota((32, 512), 0) == (named & 31), 1.0, 0.0).astype(BF16)
+    table = lax.dot_general(high, low, NT_DIMS, preferred_element_type=F32).astype(BF16)
+    sub, pool = iota((32, 768), 0), iota((32, 768), 1)
+    table = dot(table, jnp.where(sub == (pool & 31), 1.0, 0.0).astype(BF16))
+    kept = jnp.sum(jnp.where(sub == (pool >> 5), table, 0.0), axis=0, keepdims=True)
     target = (blocks >> 3) * 8 + window
-    chosen = jnp.where((iota((128, 768), 0) == target) & (kept > 0.5), 1.0, 0.0)
-    before = jnp.where(iota((768, 768), 0) < iota((768, 768), 1), 1.0, 0.0).astype(BF16)
-    rank = jnp.sum(chosen * dot(chosen.astype(BF16), before), axis=0, keepdims=True)
-    slot = jnp.where(kept > 0.5, target * 6 + rank.astype(I32), -1)
-    place[...] = jnp.where(iota((768, 768), 0) == slot, 1.0, 0.0).astype(BF16)
+    before = jnp.where(
+        (iota((128, 256), 0) < iota((128, 256), 1)), 1.0, 0.0
+    ).astype(BF16)
+    ranks, carried = [], jnp.zeros((128, 128), F32)
+    for i in range(6):
+        part = slice(i * 128, i * 128 + 128)
+        chosen = jnp.where((iota((128, 128), 0) == target[:, part]) & (kept[:, part] > 0.5), 1.0, 0.0)
+        counts = dot(chosen.astype(BF16), before)
+        ranks.append(jnp.sum(chosen * (counts[:, 0:128] + carried), axis=0, keepdims=True))
+        carried = carried + counts[:, 128:256]
+    rank = jnp.concatenate(ranks, axis=1)
+    slots[...] = jnp.where(kept > 0.5, target * 6 + rank.astype(I32), -1)
 
     row = iota((16, 768), 0)
     meta = jnp.where(row == 0, (blocks & 7).astype(F32), 0.0)
@@ -106,19 +117,7 @@
     meta = jnp.where(row == 2, as_row(w_in).astype(F32), meta)
     meta = jnp.where(row == 3, as_row(y_in).astype(F32), meta)
     meta = jnp.where(row == 4, (offset & 15).astype(F32), meta)
-    meta = lax.dot_general(meta.astype(BF16), place[...], NT_DIMS, preferred_element_type=F32)
-    rho_slot[...] = lax.dot_general(
-        meta.astype(BF16), jnp.where(iota((16, 128), 0) == 4, 1.0, 0.0).astype(BF16), TN_DIMS,
-        preferred_element_type=F32,
-    ).astype(I32)
-    lane = iota((1, 128), 1)
-    for i in range(16):
-        part = meta if i == 0 else pltpu.roll(meta, 768 - 48 * i, 1)
-        part = part[:, :128]
-        msend[i, 0:1, :] = jnp.where(
-            lane < 64, part[0:1] * 64.0 + part[1:2], pltpu.roll(part[2:3], 64, 1)
-        )
-        msend[i, 1:2, :] = part[2:3] * part[3:4]
+    metas[...] = meta.astype(BF16)
 
     pl.semaphore_wait(barrier, 22)
 
@@ -136,16 +135,37 @@
 
     jac_copy.wait()
     pl.semaphore_wait(entered, 7)
+
+    def send_prior(d, carry):
+        t = tm_at(d)
+        pltpu.make_async_remote_copy(
+            src_ref=psend.at[t], dst_ref=sig.at[m], send_sem=ps_sem, recv_sem=p_sem,
+            device_id=(r, t), device_id_type=MESH,
+        ).start()
+        return carry
+
+    lax.fori_loop(1, 8, send_prior, 0)
     own = m
-    local_meta = pltpu.make_async_copy(msend.at[r], mrecv.at[own], m_sem.at[0])
-    local_meta.start()
-
+    lane = iota((1, 128), 1)
     lanes = iota((16, 128), 1) >> 4
 
     def deliver(g, carry):
         to = [region_at(g // 4 + 2 * k, g % 4 + 2 * k) for k in range(2)]
-        at = [pl.multiple_of(t * 48, 16) for t in to]
-        which = jnp.concatenate([place[pl.ds(a, 48), :] for a in at], axis=0)
+        which = jnp.concatenate(
+            [jnp.where(iota((48, 768), 0) + t * 48 == slots[...], 1.0, 0.0) for t in to], axis=0
+        ).astype(BF16)
+        meta = lax.dot_general(metas[...], which, NT_DIMS, preferred_element_type=F32)
+        rho_slot[...] = lax.dot_general(
+            meta.astype(BF16), jnp.where(iota((16, 128), 0) == 4, 1.0, 0.0).astype(BF16), TN_DIMS,
+            preferred_element_type=F32,
+        ).astype(I32)
+        meta = jnp.concatenate([meta, jnp.zeros((16, 32), F32)], axis=1)
+        for k in range(2):
+            part = meta if k == 0 else pltpu.roll(meta, 128 - 48, 1)
+            msend[g * 2 + k, 0:1, :] = jnp.where(
+                lane < 64, part[0:1] * 64.0 + part[1:2], pltpu.roll(part[2:3], 64, 1)
+            )
+            msend[g * 2 + k, 1:2, :] = part[2:3] * part[3:4]
         for l in range(0, 2048, 256):
             picked[:, l : l + 256] = dot(which, jac[:, l : l + 256])
         for k in range(2):
@@ -153,7 +173,7 @@
             def turn(i, carry, k=k):
                 rows = pl.ds(pl.multiple_of(k * 48 + i * 16, 16), 16)
                 out = pl.ds(pl.multiple_of(i * 16, 16), 16)
-                rho = rho_slot[pl.ds(pl.multiple_of(at[k] + i * 16, 16), 16), :]
+                rho = rho_slot[rows, :]
                 parts = [picked[rows, l * 128 : (l + 1) * 128] for l in range(16)]
                 for s in (1, 2, 4, 8):
                     bit = (rho & s) != 0
@@ -175,10 +195,10 @@
             lax.fori_loop(0, 3, turn, 0)
 
         def send(k, d):
-            t = tm_at(d)
+            t = tm_at((3 * d) % 8)
             here = g * 16 + k * 8 + m
             pltpu.make_async_remote_copy(
-                src_ref=msend.at[to[k]], dst_ref=mrecv.at[here], send_sem=ms_sem, recv_sem=m_sem.at[g],
+                src_ref=msend.at[g * 2 + k], dst_ref=mrecv.at[here], send_sem=ms_sem, recv_sem=m_sem.at[g],
                 device_id=(to[k], t), device_id_type=MESH,
             ).start()
             pltpu.make_async_remote_copy(
@@ -201,17 +221,9 @@
 
     lax.fori_loop(0, 8, deliver, 0)
     local_rows = pltpu.make_async_copy(xs.at[own], rbuf.at[own], r_sem.at[0])
+    local_meta = pltpu.make_async_copy(msend.at[0], mrecv.at[own], m_sem.at[0])
     local_rows.start()
-
-    def send_prior(d, carry):
-        t = tm_at(d)
-        pltpu.make_async_remote_copy(
-            src_ref=psend.at[t], dst_ref=sig.at[m], send_sem=ps_sem, recv_sem=p_sem,
-            device_id=(r, t), device_id_type=MESH,
-        ).start()
-        return carry
-
-    lax.fori_loop(1, 8, send_prior, 0)
+    local_meta.start()
 
     factor_copy.wait()
     product = lax.dot_general(factor[...], factor[...], NT_DIMS, precision=HIGH, preferred_element_type=F32)
@@ -407,12 +419,17 @@
         pltpu.make_async_copy(seven, seven, fs_sem.at[k]).wait()
 
 
+def hand_on(x_in, r_in, x_out, r_out):
+    x_out[...] = x_in[...]
+    r_out[...] = r_in[...]
+
+
 def local(jacobian, foot_block, foot_time, obs_weight, misfit, kept_list, kept_count, prior_std, time_factor):
     field = jax.ShapeDtypeStruct(prior_std.shape, F32)
     vmem = pl.BlockSpec(memory_space=pltpu.VMEM)
     hbm = pl.BlockSpec(memory_space=pltpu.HBM)
     dma = pltpu.SemaphoreType.DMA
-    return pl.pallas_call(
+    fields = pl.pallas_call(
         kernel,
         out_shape=(field, field),
         in_specs=[vmem] * 5 + [pl.BlockSpec(memory_space=pltpu.SMEM)] + [hbm] * 3,
@@ -422,9 +439,10 @@
             pltpu.VMEM((56, 8, 128), F32),
             pltpu.VMEM((448, 448), F32),
             pltpu.VMEM((896, 448), BF16),
+            pltpu.VMEM((1, 768), I32),
+            pltpu.VMEM((16, 768), BF16),
             pltpu.VMEM((768, 768), BF16),
-            pltpu.VMEM((768, 768), BF16),
-            pltpu.VMEM((768, 128), I32),
+            pltpu.VMEM((96, 128), I32),
             pltpu.VMEM((96, 2048), F32),
             pltpu.VMEM((128, 48, 256), BF16),
             pltpu.VMEM((128, 48, 256), BF16),
@@ -453,6 +471,9 @@
             collective_id=0, has_side_effects=True, vmem_limit_bytes=60 * 2**20
         ),
     )(foot_block, foot_time, obs_weight, misfit, kept_list, kept_count, jacobian, prior_std, time_factor)
+    return pl.pallas_call(
+        hand_on, out_shape=(field, field), in_specs=[vmem, vmem], out_specs=(vmem, vmem)
+    )(*fields)
 
 
 def solution(mesh):

time: 90.5 us -> 86.4 us (0.955)
  local copies, waits for them, and re-layouts: 3.28 us -> 0 us
    unnamed x2 -> x0, local copies, waits for them, and re-layouts: 3.28 us -> none
    pallas_call x1, Pallas kernels: 85.8 us -> 83.1 us  [local(): pl.pallas_call(kernel, out_shape=(field, field), in_specs=[vmem] * 5 + [p...]
    pallas_call x0 -> x1, Pallas kernels: none -> 1.83 us  [local(): pl.pallas_call(hand_on, out_shape=(field, field), in_specs=[vmem, vmem],...]
where the time goes in v4:
time: 86.4 us; the launch traced here: 86.2 us
  Pallas kernels  84.9 us (98%)
  between operations  1.29 us (1%)
    pallas_call x1, Pallas kernels, local(): pl.pallas_call(kernel, out_shape=(field, field), in_specs=[vmem] * 5 + [p...  83.1 us
    pallas_call x1, Pallas kernels, local(): pl.pallas_call(hand_on, out_shape=(field, field), in_specs=[vmem, vmem],...  1.83 us

profile of v4, /device:TPU:1, one launch (start us, length us, event | category | flops | bytes accessed | tf_op | source)
XLA Modules:
  0.0 86.2 jit_solution(12654545117787491143)
XLA Ops:
  1.3 83.1 %shard_map.104 = (f32[56,8,128]{2,1,0:T(8,128)}, f32[56,8,128]{2,1,0:T(8,128)}) custom-call(s32[768]{0:T(1024)} %fb_in.1, s32[768]{0:T(1024)} %ft_in.1, bf16[768]{0:T(1024)(128)(2,1)} %w_in.1, bf16[768]{0:T(1024)(128)(2,1)} %y_in.1, s32[512]{0:T(512)} %list_in.1, s32[1]{0:T(128)S(6)} %copy.11.count_in, bf16[768,2048]{1,0:T(8,128)(2,1)} %jac_in.1, ...), custom_call_target="tpu_custom_call" | custom-call | tf_op jit(solution)/shard_map/pallas_call | solution.py:432
  84.4 1.8 %shard_map.105 = (f32[56,8,128]{2,1,0:T(8,128)}, f32[56,8,128]{2,1,0:T(8,128)}) custom-call(f32[56,8,128]{2,1,0:T(8,128)} %get-tuple-element.4.x_in, f32[56,8,128]{2,1,0:T(8,128)} %get-tuple-element.5.r_in), custom_call_target="tpu_custom_call" | custom-call | tf_op jit(solution)/shard_map/pallas_call | solution.py:474

commit v5 on v4

--- a/solution.py
+++ b/solution.py
@@ -50,7 +50,7 @@
 def kernel(
     fb_in, ft_in, w_in, y_in, list_in, count_in, jac_in, prior_in, factor_in,
     x_out, r_out,
-    jac, prior, factor, factor_t, slots, metas, order, rho_slot, picked, xs, rbuf, msend, mrecv, jw,
+    jac, prior, factor, factor_t, slots, metas, order, rho_slot, picked, xs, rbuf, msend, mrecv, jw, jwt,
     psend, sig, cov, key, wgt, wy, uval, ubuf, vec,
     ss, gs, scal, scal_in, fsend, fbuf, ptmp,
     entered, in_sem, s_sem, ms_sem, r_sem, m_sem, ps_sem, p_sem, us_sem, u_sem, cs_sem, c_sem, fs_sem, f_sem,
@@ -192,10 +192,11 @@
                         xs[g * 16 + k * 8 + n, out, half * 128 : (half + 1) * 128] = v[n].astype(BF16)
                 return carry
 
-            lax.fori_loop(0, 3, turn, 0)
+            for i in range(3):
+                turn(i, 0)
 
         def send(k, d):
-            t = tm_at((3 * d) % 8)
+            t = tm_at((3 * d + 4 * k) % 8)
             here = g * 16 + k * 8 + m
             pltpu.make_async_remote_copy(
                 src_ref=msend.at[g * 2 + k], dst_ref=mrecv.at[here], send_sem=ms_sem, recv_sem=m_sem.at[g],
@@ -297,7 +298,12 @@
                 for h in range(2):
                     cells.append(ss[w * 7 + 2 * a + 2 + h] if 2 * a + 2 + h < 7 else zero)
                 rows.append(jnp.concatenate(cells, axis=1))
-            v = lax.dot_general(split(jnp.concatenate(rows, axis=0)), jw[w], NT_DIMS, preferred_element_type=F32)
+            if phase == 0:
+                turned = jnp.transpose(jw[w])
+                jwt[w] = turned
+            else:
+                turned = jwt[w]
+            v = dot(split(jnp.concatenate(rows, axis=0)), turned)
             v = v[:24] + v[24:]
             for j in range(6):
                 uval[phase, pl.ds(w * 6 + j, 1), :] = jnp.sum(
@@ -319,7 +325,8 @@
                 ).start()
                 return carry
 
-            lax.fori_loop(1, 8, send_values, 0)
+            for d in range(1, 8):
+                send_values(d, 0)
             ubuf[phase, half, m] = uval[phase, half * 24 : half * 24 + 24, :]
 
     def collect(phase):
@@ -340,6 +347,8 @@
                 term = jnp.sum(term, axis=0, keepdims=True)
                 at = slice(2 * phase + i, 2 * phase + i + 1)
                 scal[at, :] = term if half == 0 else scal[at, :] + term
+            if phase == 1 and half == 1:
+                send_sums()
 
         return ready
 
@@ -354,12 +363,21 @@
             ).start()
             return carry
 
-        lax.fori_loop(1, 8, send, 0)
+        for d in range(1, 8):
+            send(d, 0)
         fbuf[k, m] = fsend[k, m]
 
     def wait_field(k):
         seven = fbuf.at[k, pl.ds(0, 7)]
         pltpu.make_async_copy(seven, seven, f_sem.at[k]).wait()
+
+    def send_sums():
+        scal_in[r] = scal[...]
+        for i in range(1, 16):
+            pltpu.make_async_remote_copy(
+                src_ref=scal, dst_ref=scal_in.at[r], send_sem=cs_sem, recv_sem=c_sem,
+                device_id=(region_at(i // 4, i % 4), m), device_id_type=MESH,
+            ).start()
 
     scal[4:8, :] = jnp.zeros((4, 128), F32)
     gs[0] = spread(wy, lambda half: None)
@@ -371,16 +389,6 @@
     gs[2] = spread(vec.at[1], collect(1))
     send_field(2)
 
-    scal_in[r] = scal[...]
-
-    def send_scal(i, carry):
-        pltpu.make_async_remote_copy(
-            src_ref=scal, dst_ref=scal_in.at[r], send_sem=cs_sem, recv_sem=c_sem,
-            device_id=(region_at(i // 4, i % 4), m), device_id_type=MESH,
-        ).start()
-        return carry
-
-    lax.fori_loop(1, 16, send_scal, 0)
     fifteen = scal_in.at[pl.ds(0, 15)]
     pltpu.make_async_copy(fifteen, fifteen, c_sem).wait()
     sums = scal_in[0]
@@ -449,6 +457,7 @@
             pltpu.VMEM((16, 2, 128), F32),
             pltpu.VMEM((128, 2, 128), F32),
             pltpu.VMEM((8, 768, 512), BF16),
+            pltpu.VMEM((8, 512, 768), BF16),
             pltpu.VMEM((8, 56, 128), F32),
             pltpu.VMEM((8, 56, 128), F32),
             pltpu.VMEM((896, 448), BF16),

time: 86.4 us -> 82.6 us (0.956)
  Pallas kernels: 84.9 us -> 81.1 us
    pallas_call x1, Pallas kernels: 83.1 us -> 79.3 us  [local(): pl.pallas_call(kernel, out_shape=(field, field), in_specs=[vmem] * 5 + [p...]
where the time goes in v5:
time: 82.6 us; the launch traced here: 82.4 us
  Pallas kernels  81.1 us (98%)
  between operations  1.29 us (2%)
    pallas_call x1, Pallas kernels, local(): pl.pallas_call(kernel, out_shape=(field, field), in_specs=[vmem] * 5 + [p...  79.3 us
    pallas_call x1, Pallas kernels, local(): pl.pallas_call(hand_on, out_shape=(field, field), in_specs=[vmem, vmem],...  1.83 us

profile of v5, /device:TPU:1, one launch (start us, length us, event | category | flops | bytes accessed | tf_op | source)
XLA Modules:
  0.0 82.4 jit_solution(14642699073362902319)
XLA Ops:
  1.3 79.3 %shard_map.104 = (f32[56,8,128]{2,1,0:T(8,128)}, f32[56,8,128]{2,1,0:T(8,128)}) custom-call(s32[768]{0:T(1024)} %fb_in.1, s32[768]{0:T(1024)} %ft_in.1, bf16[768]{0:T(1024)(128)(2,1)} %w_in.1, bf16[768]{0:T(1024)(128)(2,1)} %y_in.1, s32[512]{0:T(512)} %list_in.1, s32[1]{0:T(128)S(6)} %copy.11.count_in, bf16[768,2048]{1,0:T(8,128)(2,1)} %jac_in.1, ...), custom_call_target="tpu_custom_call" | custom-call | tf_op jit(solution)/shard_map/pallas_call | solution.py:440
  80.6 1.8 %shard_map.105 = (f32[56,8,128]{2,1,0:T(8,128)}, f32[56,8,128]{2,1,0:T(8,128)}) custom-call(f32[56,8,128]{2,1,0:T(8,128)} %get-tuple-element.4.x_in, f32[56,8,128]{2,1,0:T(8,128)} %get-tuple-element.5.r_in), custom_call_target="tpu_custom_call" | custom-call | tf_op jit(solution)/shard_map/pallas_call | solution.py:483

commit v6 on v5

--- a/solution.py
+++ b/solution.py
@@ -29,7 +29,7 @@
     for s in (1, 2, 4):
         sub_bit, lane_bit = (sub & s) != 0, (grp & s) != 0
         up = pltpu.roll(pltpu.roll(x, 8 - s, 1), 16 * s, 2)
-        down = pltpu.roll(pltpu.roll(x, s, 1), 128 - 16 * s, 2)
+        down = up if s == 4 else pltpu.roll(pltpu.roll(x, s, 1), 128 - 16 * s, 2)
         x = jnp.where(sub_bit == lane_bit, x, jnp.where(lane_bit, up, down))
     return x
 

time: 82.6 us -> 82.6 us (level)
  no operation moved by 1% of the time
where the time goes in v6:
time: 82.6 us; the launch traced here: 82.4 us
  Pallas kernels  81.1 us (98%)
  between operations  1.29 us (2%)
    pallas_call x1, Pallas kernels, local(): pl.pallas_call(kernel, out_shape=(field, field), in_specs=[vmem] * 5 + [p...  79.3 us
    pallas_call x1, Pallas kernels, local(): pl.pallas_call(hand_on, out_shape=(field, field), in_specs=[vmem, vmem],...  1.83 us

profile of v6, /device:TPU:1, one launch (start us, length us, event | category | flops | bytes accessed | tf_op | source)
XLA Modules:
  0.0 82.4 jit_solution(14642699073362902319)
XLA Ops:
  1.3 79.3 %shard_map.104 = (f32[56,8,128]{2,1,0:T(8,128)}, f32[56,8,128]{2,1,0:T(8,128)}) custom-call(s32[768]{0:T(1024)} %fb_in.1, s32[768]{0:T(1024)} %ft_in.1, bf16[768]{0:T(1024)(128)(2,1)} %w_in.1, bf16[768]{0:T(1024)(128)(2,1)} %y_in.1, s32[512]{0:T(512)} %list_in.1, s32[1]{0:T(128)S(6)} %copy.11.count_in, bf16[768,2048]{1,0:T(8,128)(2,1)} %jac_in.1, ...), custom_call_target="tpu_custom_call" | custom-call | tf_op jit(solution)/shard_map/pallas_call | solution.py:440
  80.6 1.8 %shard_map.105 = (f32[56,8,128]{2,1,0:T(8,128)}, f32[56,8,128]{2,1,0:T(8,128)}) custom-call(f32[56,8,128]{2,1,0:T(8,128)} %get-tuple-element.4.x_in, f32[56,8,128]{2,1,0:T(8,128)} %get-tuple-element.5.r_in), custom_call_target="tpu_custom_call" | custom-call | tf_op jit(solution)/shard_map/pallas_call | solution.py:483
